TPU v7x, 512 devices: a whole 4x4x16 slice. The times are simulated.
512 devices in a mesh: shot: 8 (over x, core), brick: 64 (over z, y).
Axes of the slice: x: 4, y: 4, z: 16, core: 2. Of those that a mesh axis runs over, the one named last changes fastest.
Arguments:
- adjoint_prev: float32 [16, 512, 64, 256], P('shot', 'brick'), may hold values from -6 to 6
- adjoint_now: float32 [16, 512, 64, 256], P('shot', 'brick'), may hold values from -6 to 6
- forward_snaps: bfloat16 [16, 2, 512, 64, 256], P('shot', None, 'brick'), may hold values from -6 to 6
- courant: float32 [512, 64, 256], P('brick'), may hold values from 0.05 to 0.2
- traces: float32 [16, 2, 256], P('shot'), may hold values from -12 to 12
- rec_x: int32 [16, 256], P('shot'), may hold values from 0 to 511
- rec_y: int32 [16, 256], P('shot'), may hold values from 0 to 255
- water_rows: int32 [512, 256], P('brick'), may hold values from 0 to 16
- direction: float32 [512, 64, 256], P('brick'), may hold values from -6 to 6
Outputs:
- gradient: float32 [512, 64, 256], P('brick', 'shot')
- step_sums: float32 [2], replicated
All inputs are finite; a program needn't handle non-finite values.
Results may differ from a plain program's by a relative error of at most 0.002.
Values sent between devices are 32-bit elements; how exact they have to be, the bound alone decides.
No kernel may reach another device: no remote copies, remote signals or barrier semaphores. Data moves between devices by JAX's collectives and lax.ppermute only.
A program may use at most 64 MiB of HBM per device.

v0:
```python
import jax
import jax.numpy as jnp
from jax import lax
from jax.sharding import PartitionSpec as P

far_coef = -1.0 / 12.0
near_coef = 4.0 / 3.0
center_coef = -2.5
receiver_depth = 2
water_level = 0.1


def extended(cells, sides, width):
    for axis, dim in sides:
        count = lax.axis_size(axis)
        ends = count - 1
        head = lax.slice_in_dim(cells, 0, width, axis=dim)
        tail = lax.slice_in_dim(cells, cells.shape[dim] - width, cells.shape[dim], axis=dim)
        cells = jnp.concatenate(
            [
                lax.ppermute(tail, axis, [(i, (i + 1) % count) for i in range(ends)]),
                cells,
                lax.ppermute(head, axis, [((i + 1) % count, i) for i in range(ends)]),
            ],
            axis=dim,
        )
    return cells


def laplace(ext):
    inner = ext[..., 2:-2, :, :]
    along_x = far_coef * (ext[..., 0:-4, :, :] + ext[..., 4:, :, :]) + near_coef * (
        ext[..., 1:-3, :, :] + ext[..., 3:-1, :, :]
    )
    widths = [(0, 0)] * (inner.ndim - 2) + [(2, 2), (2, 2)]
    padded = jnp.pad(inner, widths)
    along_z = far_coef * (padded[..., 0:-4, 2:-2] + padded[..., 4:, 2:-2]) + near_coef * (
        padded[..., 1:-3, 2:-2] + padded[..., 3:-1, 2:-2]
    )
    along_y = far_coef * (padded[..., 2:-2, 0:-4] + padded[..., 2:-2, 4:]) + near_coef * (
        padded[..., 2:-2, 1:-3] + padded[..., 2:-2, 3:-1]
    )
    return along_x + along_z + along_y + 3.0 * center_coef * inner


def inject(trace, row_x, row_y, first_row, rows, depth_cells, cells_y):
    hits_x = (
        row_x[:, :, None] == first_row + jnp.arange(rows, dtype=jnp.int32)[None, None, :]
    ).astype(jnp.float32)
    hits_y = (row_y[:, :, None] == jnp.arange(cells_y, dtype=jnp.int32)[None, None, :]).astype(
        jnp.float32
    )
    plane = jnp.einsum(
        "srx,sry->sxy", hits_x * trace[:, :, None], hits_y, precision=lax.Precision.HIGHEST
    )
    level = (jnp.arange(depth_cells, dtype=jnp.int32) == receiver_depth).astype(jnp.float32)
    return plane[:, :, None, :] * level[None, None, :, None]


def advance(prev, now, courant):
    ext = extended(now, (("brick", 1),), 2)
    return 2.0 * now - prev + courant * laplace(ext)


def per_device(
    adjoint_prev, adjoint_now, forward_snaps, courant, traces, rec_x, rec_y, water_rows, direction
):
    cells_x = adjoint_now.shape[1]
    depth_cells = adjoint_now.shape[2]
    cells_y = adjoint_now.shape[3]
    start = lax.axis_index("brick") * cells_x
    first = advance(adjoint_prev, adjoint_now, courant) + inject(
        traces[:, 0], rec_x, rec_y, start, cells_x, depth_cells, cells_y
    )
    second = advance(adjoint_now, first, courant) + inject(
        traces[:, 1], rec_x, rec_y, start, cells_x, depth_cells, cells_y
    )
    snap0 = forward_snaps[:, 0].astype(jnp.float32)
    snap1 = forward_snaps[:, 1].astype(jnp.float32)
    image = jnp.sum(snap0 * first + snap1 * second, axis=0)
    illum = jnp.sum(snap0 * snap0 + snap1 * snap1, axis=0)
    image_part, illum_part = (
        lax.psum_scatter(image, "shot", scatter_dimension=1, tiled=True),
        lax.psum_scatter(illum, "shot", scatter_dimension=1, tiled=True),
    )
    rows_part = image_part.shape[1]
    offset = lax.axis_index("shot") * rows_part
    peak = lax.pmax(jnp.max(illum_part), ("shot", "brick"))
    depth = offset + jnp.arange(rows_part, dtype=jnp.int32)
    keep = depth[None, :, None] >= water_rows[:, None, :]
    gradient = jnp.where(keep, image_part / (illum_part + water_level * peak), jnp.float32(0.0))
    guide = lax.dynamic_slice_in_dim(direction, offset, rows_part, 1)
    total_sq, total_dir = lax.psum(
        (jnp.sum(gradient * gradient), jnp.sum(gradient * guide)), ("shot", "brick")
    )
    return (gradient, jnp.stack([total_sq, total_dir]))


def solution(mesh):
    in_specs = (
        P("shot", "brick", None, None),
        P("shot", "brick", None, None),
        P("shot", None, "brick", None, None),
        P("brick", None, None),
        P("shot", None, None),
        P("shot", None),
        P("shot", None),
        P("brick", None),
        P("brick", None, None),
    )
    out_specs = (P("brick", "shot", None), P())
    return jax.shard_map(
        per_device, mesh=mesh, in_specs=in_specs, out_specs=out_specs, check_vma=False
    )
```

profile of v0, /device:TPU:1, one launch (start us, length us, event | category | flops | bytes accessed | tf_op | source)
XLA Modules:
  0.0 303.7 jit_solution(15388857895251218492)
XLA Ops:
  7.2 0.0 reduce-scatter.5.cloned.1.call-start
  7.2 1.2 fusion.61
  8.4 4.0 %collective-permute-start = (f32[2,2,64,256]{3,2,1,0:T(8,128)S(1)}, f32[2,2,64,256]{3,2,1,0:T(8,128)S(1)}, u32[]{:S(2)}, u32[]{:S(2)}) collective-permute-start(f32[2,2,64,256]{3,2,1,0:T(8,128)S(1)} %get-tuple-element.13), channel_id=1, source_target_pairs={{0,1},{1,2},{2,3},{3,4},{4,5},{5,6},{6,7},{7,8},{8,9},{9,10},{10,1... | collective-permute-start | bytes 786440 | tf_op jit(solution)/shard_map/ppermute | solution.py:21
  12.4 1.3 collective-permute-start.1
  13.8 0.8 fusion.62
  14.5 1.0 fusion.47
  15.6 0.2 collective-permute-done
  15.8 0.2 constant_dynamic-update-slice_fusion
  16.0 3.5 %collective-permute-done.1 = f32[2,2,64,256]{3,2,1,0:T(8,128)S(1)} collective-permute-done((f32[2,2,64,256]{3,2,1,0:T(8,128)S(1)}, f32[2,2,64,256]{3,2,1,0:T(8,128)S(1)}, u32[]{:S(2)}, u32[]{:S(2)}) %collective-permute-start.1) | collective-permute-done | bytes 262176 | tf_op jit(solution)/shard_map/ppermute | solution.py:23
  19.6 1.6 fusion.23
  21.3 5.0 %collective-permute-start.2 = (f32[2,2,64,256]{3,2,1,0:T(8,128)S(1)}, f32[2,2,64,256]{3,2,1,0:T(8,128)S(1)}, u32[]{:S(2)}, u32[]{:S(2)}) collective-permute-start(f32[2,2,64,256]{3,2,1,0:T(8,128)S(1)} %get-tuple-element.9), channel_id=1, source_target_pairs={{0,1},{1,2},{2,3},{3,4},{4,5},{5,6},{6,7},{7,8},{8,9},{9,10},{10,1... | collective-permute-start | bytes 786440 | tf_op jit(solution)/shard_map/ppermute | solution.py:21
  26.3 1.3 collective-permute-start.3
  27.6 0.3 fusion.46
  28.0 2.0 collective-permute-done.2
  30.0 3.8 %collective-permute-done.3 = f32[2,2,64,256]{3,2,1,0:T(8,128)S(1)} collective-permute-done((f32[2,2,64,256]{3,2,1,0:T(8,128)S(1)}, f32[2,2,64,256]{3,2,1,0:T(8,128)S(1)}, u32[]{:S(2)}, u32[]{:S(2)}) %collective-permute-start.3) | collective-permute-done | bytes 262176 | tf_op jit(solution)/shard_map/ppermute | solution.py:23
  33.9 3.5 %fusion.14 = (f32[8,64,256]{2,1,0:T(8,128)}, f32[8,64,256]{2,1,0:T(8,128)}) fusion(bf16[2,2,8,64,256]{4,3,2,1,0:T(8,128)(2,1)S(1)} %copy-done.3, f32[64]{0:T(128)S(1)} %compare_convert_fusion, f32[2,8,256]{2,1,0:T(8,128)S(1)} %fusion.46, f32[2,8,64,256]{3,2,1,0:T(8,128)S(1)} %fusion.23, f32[2,2,64,256]{3,2,1,0:T(8,128)S(1)} %collective-permute-done.3, ...), kind=kLoop, calls=%fused_computation.38 | loop fusion | flops 9961472 | bytes 5259520 | tf_op jit(solution)/shard_map/reduce_sum | solution.py:81
  37.3 0.0 reduce-scatter.3.cloned.1.call-start
  37.4 0.7 reduce-scatter.3.cloned.1.call-update
  38.1 47.0 %reduce-scatter.5.cloned.1.call-done = f32[8,8,256]{2,1,0:T(8,128)} async-done(((f32[8,64,256]{2,1,0:T(8,128)}), f32[8,8,256]{2,1,0:T(8,128)}) %reduce-scatter.5.cloned.1.call-update) | async-done | bytes 65552 | tf_op jit(solution)/shard_map/reduce_scatter | solution.py:84
  85.1 1.5 reduce_max.9
  86.6 105.7 %pmax.7 = f32[]{:T(128)} all-reduce(f32[]{:T(128)} %reduce_max.9), channel_id=1, replica_groups=mesh['shot'=8,'brick'=64] {'shot','brick'}, use_global_device_ids=true, to_apply=%region_5.6 | all-reduce | flops 1 | bytes 8 | tf_op jit(solution)/shard_map/pmax | solution.py:88
  193.0 2.3 multiply_reduce_fusion.1
  195.3 99.8 %all-reduce.2 = (f32[1]{0:T(128)}, f32[1]{0:T(128)}) all-reduce(f32[1]{0:T(128)} %bitcast.5, f32[1]{0:T(128)} %bitcast.4), channel_id=1, replica_groups=mesh['shot'=8,'brick'=64] {'shot','brick'}, use_global_device_ids=true, to_apply=%region_9.10 | all-reduce | flops 2 | bytes 16 | tf_op jit(solution)/shard_map/psum | solution.py:93
  295.1 1.8 pad_maximum_fusion.2
  (24 shorter events, 0.2 us)
Async XLA Ops:
  7.2 8.6 %copy-start = (f32[2,8,64,256]{3,2,1,0:T(8,128)S(1)}, f32[2,8,64,256]{3,2,1,0:T(8,128)}, u32[]{:S(2)}) copy-start(f32[2,8,64,256]{3,2,1,0:T(8,128)} %param.10) | copy-start | bytes 3145732
  7.2 77.9 %reduce-scatter.5.cloned.1.call-start = ((), (), s32[]{:S(2)}) async-start(), calls=%async_computation.3 | async-start | bytes 589824 | tf_op jit(solution)/shard_map/reduce_scatter | solution.py:84
  8.4 7.3 %collective-permute-start = (f32[2,2,64,256]{3,2,1,0:T(8,128)S(1)}, f32[2,2,64,256]{3,2,1,0:T(8,128)S(1)}, u32[]{:S(2)}, u32[]{:S(2)}) collective-permute-start(f32[2,2,64,256]{3,2,1,0:T(8,128)S(1)} %get-tuple-element.13), channel_id=1, source_target_pairs={{0,1},{1,2},{2,3},{3,4},{4,5},{5,6},{6,7},{7,8},{8,9},{9,10},{10,1... | collective-permute-start | bytes 786440 | tf_op jit(solution)/shard_map/ppermute | solution.py:21
  12.4 7.1 %collective-permute-start.1 = (f32[2,2,64,256]{3,2,1,0:T(8,128)S(1)}, f32[2,2,64,256]{3,2,1,0:T(8,128)S(1)}, u32[]{:S(2)}, u32[]{:S(2)}) collective-permute-start(f32[2,2,64,256]{3,2,1,0:T(8,128)S(1)} %get-tuple-element.14), channel_id=1, source_target_pairs={{1,0},{2,1},{3,2},{4,3},{5,4},{6,5},{7,6},{8,7},{9,8},{10,9},{11,1... | collective-permute-start | bytes 786440 | tf_op jit(solution)/shard_map/ppermute | solution.py:23
  15.8 3.8 %copy-start.1 = (f32[8,64,256]{2,1,0:T(8,128)S(1)}, f32[8,64,256]{2,1,0:T(8,128)}, u32[]{:S(2)}) copy-start(f32[8,64,256]{2,1,0:T(8,128)} %param.12) | copy-start | bytes 1572868
  15.8 3.8 %copy-start.2 = (f32[2,8,64,256]{3,2,1,0:T(8,128)S(1)}, f32[2,8,64,256]{3,2,1,0:T(8,128)}, u32[]{:S(2)}) copy-start(f32[2,8,64,256]{3,2,1,0:T(8,128)} %param.9) | copy-start | bytes 3145732
  19.6 8.0 %copy-start.5 = (s32[2,256]{1,0:T(2,128)S(1)}, s32[2,256]{1,0:T(2,128)}, u32[]{:S(2)}) copy-start(s32[2,256]{1,0:T(2,128)} %param.15) | copy-start | bytes 6148
  19.6 8.0 %copy-start.6 = (s32[2,256]{1,0:T(2,128)S(1)}, s32[2,256]{1,0:T(2,128)}, u32[]{:S(2)}) copy-start(s32[2,256]{1,0:T(2,128)} %param.14) | copy-start | bytes 6148
  21.3 12.6 %copy-start.3 = (bf16[2,2,8,64,256]{4,3,2,1,0:T(8,128)(2,1)S(1)}, bf16[2,2,8,64,256]{4,3,2,1,0:T(8,128)(2,1)}, u32[]{:S(2)}) copy-start(bf16[2,2,8,64,256]{4,3,2,1,0:T(8,128)(2,1)} %param.11) | copy-start | bytes 3145732
  21.3 8.7 %collective-permute-start.2 = (f32[2,2,64,256]{3,2,1,0:T(8,128)S(1)}, f32[2,2,64,256]{3,2,1,0:T(8,128)S(1)}, u32[]{:S(2)}, u32[]{:S(2)}) collective-permute-start(f32[2,2,64,256]{3,2,1,0:T(8,128)S(1)} %get-tuple-element.9), channel_id=1, source_target_pairs={{0,1},{1,2},{2,3},{3,4},{4,5},{5,6},{6,7},{7,8},{8,9},{9,10},{10,1... | collective-permute-start | bytes 786440 | tf_op jit(solution)/shard_map/ppermute | solution.py:21
  26.3 7.5 %collective-permute-start.3 = (f32[2,2,64,256]{3,2,1,0:T(8,128)S(1)}, f32[2,2,64,256]{3,2,1,0:T(8,128)S(1)}, u32[]{:S(2)}, u32[]{:S(2)}) collective-permute-start(f32[2,2,64,256]{3,2,1,0:T(8,128)S(1)} %get-tuple-element.10), channel_id=1, source_target_pairs={{1,0},{2,1},{3,2},{4,3},{5,4},{6,5},{7,6},{8,7},{9,8},{10,9},{11,1... | collective-permute-start | bytes 786440 | tf_op jit(solution)/shard_map/ppermute | solution.py:23
  28.0 165.0 %copy-start.4 = (s32[8,256]{1,0:T(8,128)S(1)}, s32[8,256]{1,0:T(8,128)}, u32[]{:S(2)}) copy-start(s32[8,256]{1,0:T(8,128)} %param.16) | copy-start | bytes 24580
  37.3 155.6 %reduce-scatter.3.cloned.1.call-start = ((), (), s32[]{:S(2)}) async-start(), calls=%async_computation.2 | async-start | bytes 589824 | tf_op jit(solution)/shard_map/reduce_scatter | solution.py:83
Sparse Core Ops, SparseCore 0:
  37.5 47.6 reduce-scatter.4
  88.1 37.4 reduce-scatter.2
where the time goes:
time: 304 us
  blocking collectives  206 us (68%)
  waiting for transfers between devices  57.3 us (19%)
  between operations  14.9 us (5%)
  starting transfers between devices  11.7 us (4%)
  other arithmetic  10.6 us (3%)
    pmax x1, blocking collectives, per_device(): peak = lax.pmax(jnp.max(illum_part), ('shot', 'brick'))  106 us
    psum x1, blocking collectives, per_device(): lax.psum((jnp.sum(gradient * gradient), jnp.sum(gradient * guide)), ('sho...  99.8 us
    reduce_scatter x1, waiting for transfers between devices, per_device(): lax.psum_scatter(illum, 'shot', scatter_dimension=1, tiled=True)  47 us
    ppermute x2, starting transfers between devices, extended(): lax.ppermute(tail, axis, [(i, (i + 1) % count) for i in range(ends)])  9.02 us
    ppermute x2, waiting for transfers between devices, extended(): lax.ppermute(head, axis, [((i + 1) % count, i) for i in range(ends)])  7.38 us
  transfers between devices with their start and end apart: 6, of which 5 were waited for; matrix products, arithmetic and copies ran while one was open for 1% of the time, Pallas kernels for 0%

commit v1 on v0

v1 whole, which is shorter than its diff:
```python
import functools

import jax
import jax.numpy as jnp
from jax import lax
from jax.experimental import pallas as pl
from jax.experimental.pallas import tpu as pltpu
from jax.sharding import PartitionSpec as P

far_coef = -1.0 / 12.0
near_coef = 4.0 / 3.0
receiver_depth = 2
water_level = 0.1
f32 = jnp.float32
bf16 = jnp.bfloat16


def vmem(count):
    return [pl.BlockSpec(memory_space=pltpu.VMEM)] * count


mib = 1024 * 1024
params = pltpu.CompilerParams(vmem_limit_bytes=16 * mib)


def band(size, center):
    gap = jnp.abs(
        lax.broadcasted_iota(jnp.int32, (size, size), 0)
        - lax.broadcasted_iota(jnp.int32, (size, size), 1)
    )
    weights = jnp.where(gap == 0, f32(center), f32(0.0))
    weights = jnp.where(gap == 1, f32(16.0), weights)
    return jnp.where(gap == 2, f32(-1.0), weights).astype(bf16)


def split_two(v):
    high = v.astype(bf16)
    return high, (v - high.astype(f32)).astype(bf16)


def in_plane(v, band_z, band_y):
    high, low = split_two(v)
    out = jnp.dot(band_z, high, preferred_element_type=f32)
    out += jnp.dot(band_z, low, preferred_element_type=f32)
    out += jnp.dot(high, band_y, preferred_element_type=f32)
    out += jnp.dot(low, band_y, preferred_element_type=f32)
    return out


def injected(trace, row_x, row_y, first_row, rows, cells_y):
    receivers = trace.shape[1]
    at_x = row_x == first_row + lax.broadcasted_iota(jnp.int32, (rows, receivers), 0)
    at_y = (row_y == lax.broadcasted_iota(jnp.int32, (cells_y, receivers), 0)).astype(f32)
    at_y = at_y.astype(bf16)
    rest = jnp.where(at_x, trace, f32(0.0))
    out = jnp.zeros((rows, cells_y), f32)
    for _ in range(3):
        part = rest.astype(bf16)
        rest = rest - part.astype(f32)
        out += lax.dot_general(
            part, at_y, (((1,), (1,)), ((), ())), preferred_element_type=f32
        )
    return out


def illum_kernel(snaps, core, out):
    shots, steps, planes, depth, width = snaps.shape
    parts = 2 * out.shape[1]
    rows = depth // parts
    mine = core[0]
    for i in range(planes):
        total = None
        for s in range(shots):
            for k in range(steps):
                v = snaps[s, k, i].astype(f32)
                total = v * v if total is None else total + v * v
        for p in range(parts):
            slot = (mine + p % 2) % 2
            out[slot, p // 2, i] = total[p * rows : (p + 1) * rows]


def local_kernel(
    prev, now, courant, traces, rec_x, rec_y, first_row, order, out, head, tail, plane
):
    shots, planes, depth, width = now.shape
    band_y = band(width, -90.0)
    band_z = band(depth, 0.0)
    for s in range(shots):
        plane[...] = injected(
            traces[s, 0:1], rec_x[s : s + 1], rec_y[s : s + 1], first_row[0], planes, width
        )
        for i in range(planes):
            v = now[s, i]
            total = in_plane(v, band_z, band_y)
            for gap, weight in ((1, 16.0), (2, -1.0)):
                for j in (i - gap, i + gap):
                    if 0 <= j < planes:
                        total += weight * now[s, j]
            out[s, i] = 2.0 * v - prev[s, i] + courant[i] * (total * (1.0 / 12.0))
            out[s, i, receiver_depth : receiver_depth + 1] += plane[i : i + 1]
        for j in range(2):
            head[s, j] = out[s, j]
            tail[s, j] = out[s, planes - 2 + j]
            head[shots + s, j] = now[s, j]
            tail[shots + s, j] = now[s, planes - 2 + j]
    for j in range(2):
        head[2 * shots, j] = courant[j]
        tail[2 * shots, j] = courant[planes - 2 + j]


def image_kernel(
    local, now, courant, before, after, snaps,
    traces, rec_x, rec_y, first_row, core, order, out, first, plane,
):
    shots, planes, depth, width = now.shape
    parts = 2 * out.shape[1]
    rows = depth // parts
    band_y = band(width, -90.0)
    band_z = band(depth, 0.0)
    mine = core[0]
    last = planes - 1
    for s in range(shots):
        first[s, 2] = local[s, 0] + courant[0] * (
            far_coef * before[shots + s, 0] + near_coef * before[shots + s, 1]
        )
        first[s, 3] = local[s, 1] + courant[1] * (far_coef * before[shots + s, 1])
        for i in range(2, planes - 2):
            first[s, i + 2] = local[s, i]
        first[s, planes] = local[s, last - 1] + courant[last - 1] * (far_coef * after[shots + s, 0])
        first[s, planes + 1] = local[s, last] + courant[last] * (
            near_coef * after[shots + s, 0] + far_coef * after[shots + s, 1]
        )
        first[s, 0] = before[s, 0] + before[2 * shots, 0] * (far_coef * now[s, 0])
        first[s, 1] = before[s, 1] + before[2 * shots, 1] * (
            near_coef * now[s, 0] + far_coef * now[s, 1]
        )
        first[s, planes + 2] = after[s, 0] + after[2 * shots, 0] * (
            near_coef * now[s, last] + far_coef * now[s, last - 1]
        )
        first[s, planes + 3] = after[s, 1] + after[2 * shots, 1] * (far_coef * now[s, last])
        plane[s] = injected(
            traces[s, 1:2], rec_x[s : s + 1], rec_y[s : s + 1], first_row[0], planes, width
        )
    at_level = (
        lax.broadcasted_iota(jnp.int32, (depth, width), 0) == receiver_depth
    )
    for i in range(planes):
        image = None
        for s in range(shots):
            v = first[s, i + 2]
            total = in_plane(v, band_z, band_y)
            total += 16.0 * (first[s, i + 1] + first[s, i + 3])
            total -= first[s, i] + first[s, i + 4]
            second = 2.0 * v - now[s, i] + courant[i] * (total * (1.0 / 12.0))
            second += jnp.where(at_level, plane[s, i : i + 1], f32(0.0))
            term = snaps[s, 0, i].astype(f32) * v + snaps[s, 1, i].astype(f32) * second
            image = term if image is None else image + term
        for p in range(parts):
            slot = (mine + p % 2) % 2
            out[slot, p // 2, i] = image[p * rows : (p + 1) * rows]


def folded(line, combine):
    out = line[:, :128]
    for j in range(128, line.shape[1], 128):
        out = combine(out, line[:, j : j + 128])
    return out


def peak_kernel(got, part, peak):
    total = got[0]
    for c in range(1, got.shape[0]):
        total = total + got[c]
    part[...] = total
    top = folded(jnp.max(jnp.max(total, axis=0), axis=0, keepdims=True), jnp.maximum)
    for n in range(peak.shape[0]):
        peak[n] = top


def fan_kernel(combine, got, out):
    total = got[0]
    for n in range(1, got.shape[0]):
        total = combine(total, got[n])
    for n in range(out.shape[0]):
        out[n] = total


def join_kernel(halves, received, peaks, out):
    chips, planes, rows, width = received.shape
    for c in range(chips):
        for i in range(planes):
            out[c, i] = halves[0, c, i] + received[c, i]
    top = jnp.broadcast_to(jnp.max(peaks[...], axis=0), (rows, 128))
    for c in range(chips):
        for j in range(0, width, 128):
            out[c, planes, :, j : j + 128] = top


def gradient_kernel(got, illum, water, guide, first_depth, gradient, sums):
    planes, rows, width = illum.shape
    top = got[0, planes]
    for c in range(1, got.shape[0]):
        top = jnp.maximum(top, got[c, planes])
    peak = jnp.max(top)
    depth = first_depth[0] + lax.broadcasted_iota(jnp.int32, (rows, width), 0)
    square = jnp.zeros((rows, width), f32)
    along = jnp.zeros((rows, width), f32)
    for i in range(planes):
        image = got[0, i]
        for c in range(1, got.shape[0]):
            image = image + got[c, i]
        value = image / (illum[i] + water_level * peak)
        value = jnp.where(depth >= water[i : i + 1], value, f32(0.0))
        gradient[i] = value
        square += value * value
        along += value * guide[i]
    for k, total in ((0, square), (1, along)):
        line = folded(jnp.sum(total, axis=0, keepdims=True), jnp.add)
        for n in range(sums.shape[0]):
            sums[n, :, k * 128 : (k + 1) * 128] = line


def to_next(cells):
    count = lax.axis_size("brick")
    return lax.ppermute(cells, "brick", [(i, i + 1) for i in range(count - 1)])


def to_previous(cells):
    count = lax.axis_size("brick")
    return lax.ppermute(cells, "brick", [(i + 1, i) for i in range(count - 1)])


def swapped(copies, axis, groups):
    return lax.all_to_all(copies, axis, 0, 0, axis_index_groups=groups, tiled=True)


def fan(combine, got, count):
    return pl.pallas_call(
        functools.partial(fan_kernel, combine),
        out_shape=jax.ShapeDtypeStruct((count,) + got.shape[1:], f32),
        in_specs=vmem(1),
        out_specs=vmem(1)[0],
        compiler_params=params,
        cost_estimate=pl.CostEstimate(flops=10**4, bytes_accessed=10**4, transcendentals=0),
    )(got)


def exchanged(halves):
    parts = lax.axis_size("shot")
    return lax.ppermute(halves[1], "shot", [(i, i ^ 1) for i in range(parts)])


def own_rows(halves):
    return halves[0] + exchanged(halves)


def four_chips(pieces):
    parts = lax.axis_size("shot")
    groups = [[2 * c + core for c in range(parts // 2)] for core in range(2)]
    return lax.all_to_all(pieces, "shot", 0, 0, axis_index_groups=groups, tiled=True)


def per_device(
    adjoint_prev, adjoint_now, forward_snaps, courant, traces, rec_x, rec_y, water_rows, direction
):
    now = adjoint_now
    shots, cells_x, depth_cells, cells_y = now.shape
    parts = lax.axis_size("shot")
    bricks = lax.axis_size("brick")
    rows_part = depth_cells // parts
    columns = 4
    along = [[g + columns * i for i in range(bricks // columns)] for g in range(columns)]
    across = [
        [bricks * s + columns * g + i for s in range(parts) for i in range(columns)]
        for g in range(bricks // columns)
    ]
    beside = [
        [bricks * (2 * c + core) + columns * g + i for core in range(2) for i in range(columns)]
        for c in range(parts // 2)
        for g in range(bricks // columns)
    ]
    shot = lax.axis_index("shot")
    first_row = (lax.axis_index("brick") * cells_x).astype(jnp.int32)[None]
    core = (shot % 2).astype(jnp.int32)[None]
    offset = (shot * rows_part).astype(jnp.int32)
    smem = pl.BlockSpec(memory_space=pltpu.SMEM)
    shape = jax.ShapeDtypeStruct
    halves_shape = shape((2, parts // 2, cells_x, rows_part, cells_y), f32)

    illum_halves = pl.pallas_call(
        illum_kernel,
        out_shape=halves_shape,
        in_specs=vmem(1) + [smem],
        out_specs=vmem(1)[0],
        compiler_params=params,
        cost_estimate=pl.CostEstimate(flops=10**6, bytes_accessed=2 * 10**6, transcendentals=0),
    )(forward_snaps, core)
    illum_mine = own_rows(illum_halves)
    illum_got = four_chips(illum_mine)

    illum_part, own_peak = pl.pallas_call(
        peak_kernel,
        out_shape=(
            shape((cells_x, rows_part, cells_y), f32),
            shape((len(along[0]), 1, 128), f32),
        ),
        in_specs=vmem(1),
        out_specs=tuple(vmem(2)),
        compiler_params=params,
        cost_estimate=pl.CostEstimate(flops=10**5, bytes_accessed=4 * 10**5, transcendentals=0),
    )(illum_got)
    peak = fan(jnp.maximum, swapped(own_peak, "brick", along), len(beside[0]))

    side_shape = shape((2 * shots + 1, 2, depth_cells, cells_y), f32)
    local, head, tail = pl.pallas_call(
        local_kernel,
        out_shape=(shape(now.shape, f32), side_shape, side_shape),
        in_specs=vmem(6) + [smem] + vmem(1),
        out_specs=tuple(vmem(3)),
        scratch_shapes=[pltpu.VMEM((cells_x, cells_y), f32)],
        compiler_params=params,
        cost_estimate=pl.CostEstimate(flops=10**7, bytes_accessed=4 * 10**6, transcendentals=0),
    )(adjoint_prev, now, courant, traces, rec_x, rec_y, first_row, own_peak)
    before = to_next(tail)
    after = to_previous(head)

    image_halves = pl.pallas_call(
        image_kernel,
        out_shape=halves_shape,
        in_specs=vmem(9) + [smem, smem] + vmem(1),
        out_specs=vmem(1)[0],
        scratch_shapes=[
            pltpu.VMEM((shots, cells_x + 4, depth_cells, cells_y), f32),
            pltpu.VMEM((shots, cells_x, cells_y), f32),
        ],
        compiler_params=params,
        cost_estimate=pl.CostEstimate(flops=10**7, bytes_accessed=6 * 10**6, transcendentals=0),
    )(
        local, now, courant, before, after, forward_snaps,
        traces, rec_x, rec_y, first_row, core, peak,
    )
    peaks = swapped(peak, ("shot", "brick"), beside)
    pieces = pl.pallas_call(
        join_kernel,
        out_shape=shape((parts // 2, cells_x + 1, rows_part, cells_y), f32),
        in_specs=vmem(3),
        out_specs=vmem(1)[0],
        compiler_params=params,
        cost_estimate=pl.CostEstimate(flops=10**5, bytes_accessed=10**6, transcendentals=0),
    )(image_halves, exchanged(image_halves), peaks)
    image_got = four_chips(pieces)

    guide = lax.dynamic_slice_in_dim(direction, offset, rows_part, 1)
    gradient, sums = pl.pallas_call(
        gradient_kernel,
        out_shape=(shape((cells_x, rows_part, cells_y), f32), shape((len(along[0]), 1, 256), f32)),
        in_specs=vmem(4) + [smem],
        out_specs=tuple(vmem(2)),
        compiler_params=params,
        cost_estimate=pl.CostEstimate(flops=10**6, bytes_accessed=6 * 10**5, transcendentals=0),
    )(image_got, illum_part, water_rows, guide, offset[None])
    sums = fan(jnp.add, swapped(sums, "brick", along), len(across[0]))
    sums = jnp.sum(swapped(sums, ("shot", "brick"), across), axis=0)
    return (gradient, jnp.sum(sums.reshape(2, 128), axis=1))


def solution(mesh):
    in_specs = (
        P("shot", "brick", None, None),
        P("shot", "brick", None, None),
        P("shot", None, "brick", None, None),
        P("brick", None, None),
        P("shot", None, None),
        P("shot", None),
        P("shot", None),
        P("brick", None),
        P("brick", None, None),
    )
    out_specs = (P("brick", "shot", None), P())
    return jax.shard_map(
        per_device, mesh=mesh, in_specs=in_specs, out_specs=out_specs, check_vma=False
    )
```

time: 304 us -> 109 us (0.36)
  blocking collectives: 206 us -> 61.8 us
  waiting for transfers between devices: 57.3 us -> 13.3 us
  between operations: 14.9 us -> 0.84 us
  starting transfers between devices: 11.7 us -> 24.2 us
  other arithmetic: 10.6 us -> 1.42 us
  Pallas kernels: 0 us -> 4.92 us
    pmax x1 -> x0, blocking collectives: 106 us -> none  [per_device(): peak = lax.pmax(jnp.max(illum_part), ('shot', 'brick'))]
    psum x1 -> x0, blocking collectives: 99.8 us -> none  [per_device(): lax.psum((jnp.sum(gradient * gradient), jnp.sum(gradient * guide)), ('sho...]
    all_to_all x0 -> x4, blocking collectives: none -> 61.8 us  [swapped(): lax.all_to_all(copies, axis, 0, 0, axis_index_groups=groups, tiled=True)]
    reduce_scatter x2 -> x0, waiting for transfers between devices: 47 us -> none  [the longest x1 47 us: per_device(): lax.psum_scatter(illum, 'shot', scatter_dimension=1, tiled=True)]
    all_to_all x0 -> x2, waiting for transfers between devices: none -> 12.1 us  [four_chips(): lax.all_to_all(pieces, 'shot', 0, 0, axis_index_groups=groups, tiled=True)]
    ppermute x4, waiting for transfers between devices: 9.57 us -> 1.15 us  [the longest x2 1.14 us: exchanged(): return lax.ppermute(halves[1], 'shot', [(i, i ^ 1) for i in range(parts)])]
    all_to_all x0 -> x2, starting transfers between devices: none -> 6.99 us  [four_chips(): lax.all_to_all(pieces, 'shot', 0, 0, axis_index_groups=groups, tiled=True)]
    ppermute x4, starting transfers between devices: 11.6 us -> 17.3 us  [the longest x2 14.6 us: exchanged(): return lax.ppermute(halves[1], 'shot', [(i, i ^ 1) for i in range(parts)])]
  transfers between devices with their start and end apart: 6 -> 6, of which waited for: 5 -> 3; matrix products, arithmetic and copies ran while one was open for 1% -> 0% of each run, Pallas kernels for 0% -> 0%
where the time goes in v1:
time: 109 us; the launch traced here: 108 us
  blocking collectives  61.8 us (57%)
  starting transfers between devices  24.2 us (22%)
  waiting for transfers between devices  13.3 us (12%)
  Pallas kernels  4.92 us (5%)
  local copies, waits for them, and re-layouts  2.01 us (2%)
  other arithmetic  1.42 us (1%)
    all_to_all x4, blocking collectives, swapped(): lax.all_to_all(copies, axis, 0, 0, axis_index_groups=groups, tiled=True)  61.8 us
    ppermute x2, starting transfers between devices, exchanged(): return lax.ppermute(halves[1], 'shot', [(i, i ^ 1) for i in range(parts)])  14.6 us
    all_to_all x2, waiting for transfers between devices, four_chips(): lax.all_to_all(pieces, 'shot', 0, 0, axis_index_groups=groups, tiled=True)  12.1 us
    all_to_all x2, starting transfers between devices, four_chips(): lax.all_to_all(pieces, 'shot', 0, 0, axis_index_groups=groups, tiled=True)  6.99 us
  transfers between devices with their start and end apart: 6, of which 3 were waited for; matrix products, arithmetic and copies ran while one was open for 0% of the time, Pallas kernels for 0%

profile of v1, /device:TPU:1, one launch (start us, length us, event | category | flops | bytes accessed | tf_op | source)
XLA Modules:
  0.0 108.5 jit_solution(3442971677829529297)
XLA Ops:
  0.7 1.3 %copy-done.2 = bf16[2,2,8,64,256]{4,3,2,1,0:T(8,128)(2,1)S(1)} copy-done((bf16[2,2,8,64,256]{4,3,2,1,0:T(8,128)(2,1)S(1)}, bf16[2,2,8,64,256]{4,3,2,1,0:T(8,128)(2,1)}, u32[]{:S(2)}) %copy-start.2) | copy-done | bytes 1048600
  1.9 0.1 shard_map.104
  2.1 8.9 %collective-permute-start = (f32[4,8,8,256]{3,2,1,0:T(8,128)S(1)}, f32[4,8,8,256]{3,2,1,0:T(8,128)S(1)}, u32[]{:S(2)}, u32[]{:S(2)}) collective-permute-start(f32[4,8,8,256]{3,2,1,0:T(8,128)S(1)} %slice_bitcast_fusion.1), channel_id=1, source_target_pairs={{0,64},{64,0},{128,192},{192,128},{256,320},{320,256},{384,448},{4... | collective-permute-start | bytes 786440 | tf_op jit(solution)/shard_map/ppermute | solution.py:250
  11.0 1.1 %collective-permute-done = f32[4,8,8,256]{3,2,1,0:T(8,128)S(1)} collective-permute-done((f32[4,8,8,256]{3,2,1,0:T(8,128)S(1)}, f32[4,8,8,256]{3,2,1,0:T(8,128)S(1)}, u32[]{:S(2)}, u32[]{:S(2)}) %collective-permute-start) | collective-permute-done | bytes 262176 | tf_op jit(solution)/shard_map/ppermute | solution.py:250
  12.2 0.7 fusion
  12.9 3.5 %all-to-all-start = ((f32[4,8,8,256]{3,2,1,0:T(8,128)}), f32[4,8,8,256]{3,2,1,0:T(8,128)S(1)}, u32[]{:S(2)}, u32[]{:S(2)}) async-start(f32[4,8,8,256]{3,2,1,0:T(8,128)} %fusion), calls=%async_computation | async-start | bytes 524288 | tf_op jit(solution)/shard_map/all_to_all | solution.py:260
  16.5 6.1 %all-to-all-done.got = f32[4,8,8,256]{3,2,1,0:T(8,128)S(1)} async-done(((f32[4,8,8,256]{3,2,1,0:T(8,128)}), f32[4,8,8,256]{3,2,1,0:T(8,128)S(1)}, u32[]{:S(2)}, u32[]{:S(2)}) %all-to-all-start) | async-done | bytes 262176 | tf_op jit(solution)/shard_map/all_to_all | solution.py:260
  22.6 0.6 copy-done.6
  23.3 0.0 copy-done.8
  23.3 1.5 %shard_map.106 = (f32[2,8,64,256]{3,2,1,0:T(8,128)S(1)}, f32[5,2,64,256]{3,2,1,0:T(8,128)S(1)}, f32[5,2,64,256]{3,2,1,0:T(8,128)S(1)}) custom-call(f32[2,8,64,256]{3,2,1,0:T(8,128)S(1)} %copy-done.5, f32[2,8,64,256]{3,2,1,0:T(8,128)S(1)} %copy-done.1, f32[8,64,256]{2,1,0:T(8,128)S(1)} %copy-done.4, f32[2,2,256]{2,1,0:T(2,128)S(1)} %copy-done.6, ...), custom_call_target="tpu_custom_call" | custom-call | flops 10000000 | bytes 4000000 | tf_op jit(solution)/shard_map/pallas_call | solution.py:315
  24.8 1.3 %collective-permute-start.1 = (f32[5,2,64,256]{3,2,1,0:T(8,128)S(1)}, f32[5,2,64,256]{3,2,1,0:T(8,128)S(1)}, u32[]{:S(2)}, u32[]{:S(2)}) collective-permute-start(f32[5,2,64,256]{3,2,1,0:T(8,128)S(1)} %get-tuple-element.11), channel_id=1, source_target_pairs={{0,1},{1,2},{2,3},{3,4},{4,5},{5,6},{6,7},{7,8},{8,9},{9,10},{10,1... | collective-permute-start | bytes 1966088 | tf_op jit(solution)/shard_map/ppermute | solution.py:225
  26.1 1.3 %collective-permute-start.2 = (f32[5,2,64,256]{3,2,1,0:T(8,128)S(1)}, f32[5,2,64,256]{3,2,1,0:T(8,128)S(1)}, u32[]{:S(2)}, u32[]{:S(2)}) collective-permute-start(f32[5,2,64,256]{3,2,1,0:T(8,128)S(1)} %get-tuple-element.12), channel_id=1, source_target_pairs={{1,0},{2,1},{3,2},{4,3},{5,4},{6,5},{7,6},{8,7},{9,8},{10,9},{11,1... | collective-permute-start | bytes 1966088 | tf_op jit(solution)/shard_map/ppermute | solution.py:230
  27.4 26.9 %all_to_all.30.got = f32[16,1,128]{2,1,0:T(1,128)S(1)} all-to-all(f32[16,1,128]{2,1,0:T(1,128)S(1)} %get-tuple-element.9.order), channel_id=1, replica_groups={{0,4,8,12,16,20,24,28,32,36,40,44,48,52,56,60},{1,5,9,13,17,21,25,29,33..., dimensions={0} | all-to-all | bytes 16384 | tf_op jit(solution)/shard_map/all_to_all | solution.py:234
  54.4 1.7 %shard_map.108.halves = f32[2,4,8,8,256]{4,3,2,1,0:T(8,128)S(1)} custom-call(f32[2,8,64,256]{3,2,1,0:T(8,128)S(1)} %get-tuple-element.10.local, f32[2,8,64,256]{3,2,1,0:T(8,128)S(1)} %copy-done.1, f32[8,64,256]{2,1,0:T(8,128)S(1)} %copy-done.4, f32[5,2,64,256]{3,2,1,0:T(8,128)S(1)} %collective-permute-done.1.before, ...), custom_call_target="tpu_custom_call" | custom-call | flops 10000000 | bytes 6000000 | tf_op jit(solution)/shard_map/pallas_call | solution.py:327
  56.1 5.7 %collective-permute-start.3 = (f32[4,8,8,256]{3,2,1,0:T(8,128)S(1)}, f32[4,8,8,256]{3,2,1,0:T(8,128)S(1)}, u32[]{:S(2)}, u32[]{:S(2)}) collective-permute-start(f32[4,8,8,256]{3,2,1,0:T(8,128)S(1)} %slice_bitcast_fusion), channel_id=1, source_target_pairs={{0,64},{64,0},{128,192},{192,128},{256,320},{320,256},{384,448},{4... | collective-permute-start | bytes 786440 | tf_op jit(solution)/shard_map/ppermute | solution.py:250
  61.9 6.9 %all_to_all.31.peaks = f32[8,1,128]{2,1,0:T(1,128)S(1)} all-to-all(f32[8,1,128]{2,1,0:T(1,128)S(1)} %shard_map.107.order), channel_id=1, replica_groups={{0,1,2,3,64,65,66,67},{4,5,6,7,68,69,70,71},{8,9,10,11,72,73,74,75},{12..., dimensions={0} | all-to-all | bytes 8192 | tf_op jit(solution)/shard_map/all_to_all | solution.py:234
  68.8 0.7 shard_map.109
  69.5 3.5 %all-to-all-start.3 = ((f32[4,9,8,256]{3,2,1,0:T(8,128)}), f32[4,9,8,256]{3,2,1,0:T(8,128)S(1)}, u32[]{:S(2)}, u32[]{:S(2)}) async-start(f32[4,9,8,256]{3,2,1,0:T(8,128)} %shard_map.109), calls=%async_computation.3 | async-start | bytes 589824 | tf_op jit(solution)/shard_map/all_to_all | solution.py:260
  73.0 6.0 %all-to-all-done.3.got = f32[4,9,8,256]{3,2,1,0:T(8,128)S(1)} async-done(((f32[4,9,8,256]{3,2,1,0:T(8,128)}), f32[4,9,8,256]{3,2,1,0:T(8,128)S(1)}, u32[]{:S(2)}, u32[]{:S(2)}) %all-to-all-start.3) | async-done | bytes 294944 | tf_op jit(solution)/shard_map/all_to_all | solution.py:260
  79.1 0.8 shard_map.110
  79.9 14.4 %all_to_all.32.got = f32[16,1,256]{2,1,0:T(1,128)S(1)} all-to-all(f32[16,1,256]{2,1,0:T(1,128)S(1)} %get-tuple-element.15), channel_id=1, replica_groups={{0,4,8,12,16,20,24,28,32,36,40,44,48,52,56,60},{1,5,9,13,17,21,25,29,33..., dimensions={0} | all-to-all | bytes 32768 | tf_op jit(solution)/shard_map/all_to_all | solution.py:234
  94.3 13.5 %all_to_all.33 = f32[32,1,256]{2,1,0:T(1,128)S(1)} all-to-all(f32[32,1,256]{2,1,0:T(1,128)S(1)} %shard_map.111), channel_id=1, replica_groups={{0,1,2,3,64,65,66,67,128,129,130,131,192,193,194,195,256,257,258,259,32..., dimensions={0} | all-to-all | bytes 65536 | tf_op jit(solution)/shard_map/all_to_all | solution.py:234
  107.8 0.1 reduce_sum.18
  107.9 0.6 bitcast_reduce_fusion
  (26 shorter events, 0.2 us)
Async XLA Ops:
  0.6 72.4 %copy-start = (f32[8,64,256]{2,1,0:T(8,128)S(1)}, f32[8,64,256]{2,1,0:T(8,128)}, u32[]{:S(2)}) copy-start(f32[8,64,256]{2,1,0:T(8,128)} %param.17) | copy-start | bytes 1572868
  0.7 1.3 %copy-start.2 = (bf16[2,2,8,64,256]{4,3,2,1,0:T(8,128)(2,1)S(1)}, bf16[2,2,8,64,256]{4,3,2,1,0:T(8,128)(2,1)}, u32[]{:S(2)}) copy-start(bf16[2,2,8,64,256]{4,3,2,1,0:T(8,128)(2,1)} %snaps.3) | copy-start | bytes 3145732
  1.9 20.7 %copy-start.5 = (f32[2,8,64,256]{3,2,1,0:T(8,128)S(1)}, f32[2,8,64,256]{3,2,1,0:T(8,128)}, u32[]{:S(2)}) copy-start(f32[2,8,64,256]{3,2,1,0:T(8,128)} %prev.1) | copy-start | bytes 3145732
  2.1 20.5 %copy-start.1 = (f32[2,8,64,256]{3,2,1,0:T(8,128)S(1)}, f32[2,8,64,256]{3,2,1,0:T(8,128)}, u32[]{:S(2)}) copy-start(f32[2,8,64,256]{3,2,1,0:T(8,128)} %now.3) | copy-start | bytes 3145732
  2.1 10.1 %collective-permute-start = (f32[4,8,8,256]{3,2,1,0:T(8,128)S(1)}, f32[4,8,8,256]{3,2,1,0:T(8,128)S(1)}, u32[]{:S(2)}, u32[]{:S(2)}) collective-permute-start(f32[4,8,8,256]{3,2,1,0:T(8,128)S(1)} %slice_bitcast_fusion.1), channel_id=1, source_target_pairs={{0,64},{64,0},{128,192},{192,128},{256,320},{320,256},{384,448},{4... | collective-permute-start | bytes 786440 | tf_op jit(solution)/shard_map/ppermute | solution.py:250
  12.9 9.7 %copy-start.4 = (f32[8,64,256]{2,1,0:T(8,128)S(1)}, f32[8,64,256]{2,1,0:T(8,128)}, u32[]{:S(2)}) copy-start(f32[8,64,256]{2,1,0:T(8,128)} %courant.3) | copy-start | bytes 1572868
  12.9 9.6 %all-to-all-start = ((f32[4,8,8,256]{3,2,1,0:T(8,128)}), f32[4,8,8,256]{3,2,1,0:T(8,128)S(1)}, u32[]{:S(2)}, u32[]{:S(2)}) async-start(f32[4,8,8,256]{3,2,1,0:T(8,128)} %fusion), calls=%async_computation | async-start | bytes 524288 | tf_op jit(solution)/shard_map/all_to_all | solution.py:260
  22.6 0.7 copy-start.6
  22.6 0.7 copy-start.9
  22.6 0.7 copy-start.8
  23.3 31.1 %copy-start.3 = (bf16[2,2,8,64,256]{4,3,2,1,0:T(8,128)(2,1)S(1)}, bf16[2,2,8,64,256]{4,3,2,1,0:T(8,128)(2,1)}, u32[]{:S(2)}) copy-start(bf16[2,2,8,64,256]{4,3,2,1,0:T(8,128)(2,1)} %snaps.3) | copy-start | bytes 3145732
  24.8 29.6 %collective-permute-start.1 = (f32[5,2,64,256]{3,2,1,0:T(8,128)S(1)}, f32[5,2,64,256]{3,2,1,0:T(8,128)S(1)}, u32[]{:S(2)}, u32[]{:S(2)}) collective-permute-start(f32[5,2,64,256]{3,2,1,0:T(8,128)S(1)} %get-tuple-element.11), channel_id=1, source_target_pairs={{0,1},{1,2},{2,3},{3,4},{4,5},{5,6},{6,7},{7,8},{8,9},{9,10},{10,1... | collective-permute-start | bytes 1966088 | tf_op jit(solution)/shard_map/ppermute | solution.py:225
  26.1 28.3 %collective-permute-start.2 = (f32[5,2,64,256]{3,2,1,0:T(8,128)S(1)}, f32[5,2,64,256]{3,2,1,0:T(8,128)S(1)}, u32[]{:S(2)}, u32[]{:S(2)}) collective-permute-start(f32[5,2,64,256]{3,2,1,0:T(8,128)S(1)} %get-tuple-element.12), channel_id=1, source_target_pairs={{1,0},{2,1},{3,2},{4,3},{5,4},{6,5},{7,6},{8,7},{9,8},{10,9},{11,1... | collective-permute-start | bytes 1966088 | tf_op jit(solution)/shard_map/ppermute | solution.py:230
  56.1 12.7 %collective-permute-start.3 = (f32[4,8,8,256]{3,2,1,0:T(8,128)S(1)}, f32[4,8,8,256]{3,2,1,0:T(8,128)S(1)}, u32[]{:S(2)}, u32[]{:S(2)}) collective-permute-start(f32[4,8,8,256]{3,2,1,0:T(8,128)S(1)} %slice_bitcast_fusion), channel_id=1, source_target_pairs={{0,64},{64,0},{128,192},{192,128},{256,320},{320,256},{384,448},{4... | collective-permute-start | bytes 786440 | tf_op jit(solution)/shard_map/ppermute | solution.py:250
  69.5 9.5 %all-to-all-start.3 = ((f32[4,9,8,256]{3,2,1,0:T(8,128)}), f32[4,9,8,256]{3,2,1,0:T(8,128)S(1)}, u32[]{:S(2)}, u32[]{:S(2)}) async-start(f32[4,9,8,256]{3,2,1,0:T(8,128)} %shard_map.109), calls=%async_computation.3 | async-start | bytes 589824 | tf_op jit(solution)/shard_map/all_to_all | solution.py:260
  73.0 6.1 %copy-start.7 = (s32[8,256]{1,0:T(8,128)S(1)}, s32[8,256]{1,0:T(8,128)}, u32[]{:S(2)}) copy-start(s32[8,256]{1,0:T(8,128)} %water.1) | copy-start | bytes 24580

commit v2 on v1

--- a/solution.py
+++ b/solution.py
@@ -80,7 +80,7 @@
 
 
 def local_kernel(
-    prev, now, courant, traces, rec_x, rec_y, first_row, order, out, head, tail, plane
+    prev, now, courant, traces, rec_x, rec_y, first_row, out, head, tail, plane
 ):
     shots, planes, depth, width = now.shape
     band_y = band(width, -90.0)
@@ -167,7 +167,11 @@
     return out
 
 
-def peak_kernel(got, part, peak):
+def peak_kernel(got, direction, water, first_depth, part, peak, guide, floor):
+    span = pl.ds(pl.multiple_of(first_depth[0], guide.shape[1]), guide.shape[1])
+    for i in range(guide.shape[0]):
+        guide[i] = direction[i, span]
+    floor[...] = water[...]
     total = got[0]
     for c in range(1, got.shape[0]):
         total = total + got[c]
@@ -218,6 +222,15 @@
         line = folded(jnp.sum(total, axis=0, keepdims=True), jnp.add)
         for n in range(sums.shape[0]):
             sums[n, :, k * 128 : (k + 1) * 128] = line
+
+
+def last_kernel(got, value, gradient, sums):
+    gradient[...] = value[...]
+    total = got[0]
+    for n in range(1, got.shape[0]):
+        total = total + got[n]
+    sums[0] = jnp.sum(total[:, :128])
+    sums[1] = jnp.sum(total[:, 128:])
 
 
 def to_next(cells):
@@ -298,29 +311,32 @@
     illum_mine = own_rows(illum_halves)
     illum_got = four_chips(illum_mine)
 
-    illum_part, own_peak = pl.pallas_call(
+    part_shape = shape((cells_x, rows_part, cells_y), f32)
+    illum_part, own_peak, guide, floor = pl.pallas_call(
         peak_kernel,
         out_shape=(
-            shape((cells_x, rows_part, cells_y), f32),
+            part_shape,
             shape((len(along[0]), 1, 128), f32),
+            part_shape,
+            shape(water_rows.shape, jnp.int32),
         ),
-        in_specs=vmem(1),
-        out_specs=tuple(vmem(2)),
+        in_specs=vmem(3) + [smem],
+        out_specs=tuple(vmem(4)),
         compiler_params=params,
         cost_estimate=pl.CostEstimate(flops=10**5, bytes_accessed=4 * 10**5, transcendentals=0),
-    )(illum_got)
+    )(illum_got, direction, water_rows, offset[None])
     peak = fan(jnp.maximum, swapped(own_peak, "brick", along), len(beside[0]))
 
     side_shape = shape((2 * shots + 1, 2, depth_cells, cells_y), f32)
     local, head, tail = pl.pallas_call(
         local_kernel,
         out_shape=(shape(now.shape, f32), side_shape, side_shape),
-        in_specs=vmem(6) + [smem] + vmem(1),
+        in_specs=vmem(6) + [smem],
         out_specs=tuple(vmem(3)),
         scratch_shapes=[pltpu.VMEM((cells_x, cells_y), f32)],
         compiler_params=params,
         cost_estimate=pl.CostEstimate(flops=10**7, bytes_accessed=4 * 10**6, transcendentals=0),
-    )(adjoint_prev, now, courant, traces, rec_x, rec_y, first_row, own_peak)
+    )(adjoint_prev, now, courant, traces, rec_x, rec_y, first_row)
     before = to_next(tail)
     after = to_previous(head)
 
@@ -350,7 +366,6 @@
     )(image_halves, exchanged(image_halves), peaks)
     image_got = four_chips(pieces)
 
-    guide = lax.dynamic_slice_in_dim(direction, offset, rows_part, 1)
     gradient, sums = pl.pallas_call(
         gradient_kernel,
         out_shape=(shape((cells_x, rows_part, cells_y), f32), shape((len(along[0]), 1, 256), f32)),
@@ -358,10 +373,17 @@
         out_specs=tuple(vmem(2)),
         compiler_params=params,
         cost_estimate=pl.CostEstimate(flops=10**6, bytes_accessed=6 * 10**5, transcendentals=0),
-    )(image_got, illum_part, water_rows, guide, offset[None])
+    )(image_got, illum_part, floor, guide, offset[None])
     sums = fan(jnp.add, swapped(sums, "brick", along), len(across[0]))
-    sums = jnp.sum(swapped(sums, ("shot", "brick"), across), axis=0)
-    return (gradient, jnp.sum(sums.reshape(2, 128), axis=1))
+    gradient, sums = pl.pallas_call(
+        last_kernel,
+        out_shape=(shape(gradient.shape, f32), shape((2,), f32)),
+        in_specs=vmem(2),
+        out_specs=(vmem(1)[0], smem),
+        compiler_params=params,
+        cost_estimate=pl.CostEstimate(flops=10**4, bytes_accessed=2 * 10**5, transcendentals=0),
+    )(swapped(sums, ("shot", "brick"), across), gradient)
+    return (gradient, sums)
 
 
 def solution(mesh):

time: 109 us -> 112 us (1.028)
  waiting for transfers between devices: 13.3 us -> 6.8 us
  blocking collectives: 61.8 us -> 68.1 us
  local copies, waits for them, and re-layouts: 2.01 us -> 7.09 us
  starting transfers between devices: 24.2 us -> 21 us
  Pallas kernels: 4.92 us -> 6.38 us
    all_to_all x0 -> x1, blocking collectives: none -> 8.78 us  [four_chips(): lax.all_to_all(pieces, 'shot', 0, 0, axis_index_groups=groups, tiled=True)]
    all_to_all x2 -> x1, waiting for transfers between devices: 12.1 us -> 6.79 us  [four_chips(): lax.all_to_all(pieces, 'shot', 0, 0, axis_index_groups=groups, tiled=True)]
    unnamed x20 -> x24, local copies, waits for them, and re-layouts: 1.96 us -> 6.36 us
    all_to_all x2 -> x1, starting transfers between devices: 6.99 us -> 3.54 us  [four_chips(): lax.all_to_all(pieces, 'shot', 0, 0, axis_index_groups=groups, tiled=True)]
    all_to_all x4, blocking collectives: 61.8 us -> 59.3 us  [swapped(): lax.all_to_all(copies, axis, 0, 0, axis_index_groups=groups, tiled=True)]
    pallas_call x1, Pallas kernels: 1.69 us -> 2.83 us  [per_device(): pl.pallas_call(image_kernel, out_shape=halves_shape, in_specs=vmem(9) + [...]
    ppermute x2, waiting for transfers between devices: 1.14 us -> 0.01 us  [exchanged(): return lax.ppermute(halves[1], 'shot', [(i, i ^ 1) for i in range(parts)])]
  transfers between devices with their start and end apart: 6 -> 5, of which waited for: 3 -> 1; matrix products, arithmetic and copies ran while one was open for 0% -> 1% of each run, Pallas kernels for 0% -> 2%
where the time goes in v2:
time: 112 us; the launch traced here: 111 us
  blocking collectives  68.1 us (61%)
  starting transfers between devices  21 us (19%)
  local copies, waits for them, and re-layouts  7.09 us (6%)
  waiting for transfers between devices  6.8 us (6%)
  Pallas kernels  6.38 us (6%)
    all_to_all x4, blocking collectives, swapped(): lax.all_to_all(copies, axis, 0, 0, axis_index_groups=groups, tiled=True)  59.3 us
    ppermute x2, starting transfers between devices, exchanged(): return lax.ppermute(halves[1], 'shot', [(i, i ^ 1) for i in range(parts)])  13.9 us
    all_to_all x1, blocking collectives, four_chips(): lax.all_to_all(pieces, 'shot', 0, 0, axis_index_groups=groups, tiled=True)  8.78 us
    all_to_all x1, waiting for transfers between devices, four_chips(): lax.all_to_all(pieces, 'shot', 0, 0, axis_index_groups=groups, tiled=True)  6.79 us
    unnamed x24, local copies, waits for them, and re-layouts  6.36 us
    all_to_all x1, starting transfers between devices, four_chips(): lax.all_to_all(pieces, 'shot', 0, 0, axis_index_groups=groups, tiled=True)  3.54 us
    pallas_call x1, Pallas kernels, per_device(): pl.pallas_call(image_kernel, out_shape=halves_shape, in_specs=vmem(9) + [...  2.83 us
    pallas_call x1, Pallas kernels, per_device(): pl.pallas_call(local_kernel, out_shape=(shape(now.shape, f32), side_shape...  2.48 us
  transfers between devices with their start and end apart: 5, of which 1 were waited for; matrix products, arithmetic and copies ran while one was open for 1% of the time, Pallas kernels for 2%

profile of v2, /device:TPU:1, one launch (start us, length us, event | category | flops | bytes accessed | tf_op | source)
XLA Modules:
  0.0 110.9 jit_solution(4520707264282722296)
XLA Ops:
  0.7 1.2 %copy-done.1 = bf16[2,2,8,64,256]{4,3,2,1,0:T(8,128)(2,1)S(1)} copy-done((bf16[2,2,8,64,256]{4,3,2,1,0:T(8,128)(2,1)S(1)}, bf16[2,2,8,64,256]{4,3,2,1,0:T(8,128)(2,1)}, u32[]{:S(2)}) %copy-start.1) | copy-done | bytes 1048600
  1.9 0.1 shard_map.105
  2.0 0.7 slice_bitcast_fusion.1
  2.7 8.9 %collective-permute-start.2 = (f32[4,8,8,256]{3,2,1,0:T(8,128)}, f32[4,8,8,256]{3,2,1,0:T(8,128)S(1)}, u32[]{:S(2)}, u32[]{:S(2)}) collective-permute-start(f32[4,8,8,256]{3,2,1,0:T(8,128)} %slice_bitcast_fusion.1), channel_id=1, source_target_pairs={{0,64},{64,0},{128,192},{192,128},{256,320},{320,256},{384,448},{4... | collective-permute-start | bytes 786440 | tf_op jit(solution)/shard_map/ppermute | solution.py:263
  11.7 0.6 copy-done.10
  12.3 1.2 %copy-done.4 = f32[2,8,64,256]{3,2,1,0:T(8,128)S(1)} copy-done((f32[2,8,64,256]{3,2,1,0:T(8,128)S(1)}, f32[2,8,64,256]{3,2,1,0:T(8,128)}, u32[]{:S(2)}) %copy-start.4) | copy-done | bytes 1048600
  13.6 2.5 %shard_map.104 = (f32[2,8,64,256]{3,2,1,0:T(8,128)S(1)}, f32[5,2,64,256]{3,2,1,0:T(8,128)}, f32[5,2,64,256]{3,2,1,0:T(8,128)}) custom-call(f32[2,8,64,256]{3,2,1,0:T(8,128)S(1)} %copy-done.4, f32[2,8,64,256]{3,2,1,0:T(8,128)S(1)} %copy-done, f32[8,64,256]{2,1,0:T(8,128)S(1)} %copy-done.3, f32[2,2,256]{2,1,0:T(2,128)S(1)} %copy-done.8, ...), custom_call_target="tpu_custom_call" | custom-call | flops 10000000 | bytes 4000000 | tf_op jit(solution)/shard_map/pallas_call | solution.py:331
  16.0 1.0 copy-done.5
  17.0 2.1 %collective-permute-start = (f32[5,2,64,256]{3,2,1,0:T(8,128)}, f32[5,2,64,256]{3,2,1,0:T(8,128)}, u32[]{:S(2)}, u32[]{:S(2)}) collective-permute-start(f32[5,2,64,256]{3,2,1,0:T(8,128)} %get-tuple-element.12), channel_id=1, source_target_pairs={{0,1},{1,2},{2,3},{3,4},{4,5},{5,6},{6,7},{7,8},{8,9},{9,10},{10,1... | collective-permute-start | bytes 1966088 | tf_op jit(solution)/shard_map/ppermute | solution.py:238
  19.2 1.4 %collective-permute-start.1 = (f32[5,2,64,256]{3,2,1,0:T(8,128)}, f32[5,2,64,256]{3,2,1,0:T(8,128)}, u32[]{:S(2)}, u32[]{:S(2)}) collective-permute-start(f32[5,2,64,256]{3,2,1,0:T(8,128)} %get-tuple-element.13), channel_id=1, source_target_pairs={{1,0},{2,1},{3,2},{4,3},{5,4},{6,5},{7,6},{8,7},{9,8},{10,9},{11,1... | collective-permute-start | bytes 1966088 | tf_op jit(solution)/shard_map/ppermute | solution.py:243
  20.6 0.7 fusion
  21.3 3.5 %all-to-all-start = ((f32[4,8,8,256]{3,2,1,0:T(8,128)}), f32[4,8,8,256]{3,2,1,0:T(8,128)S(1)}, u32[]{:S(2)}, u32[]{:S(2)}) async-start(f32[4,8,8,256]{3,2,1,0:T(8,128)} %fusion), calls=%async_computation | async-start | bytes 524288 | tf_op jit(solution)/shard_map/all_to_all | solution.py:273
  24.9 6.8 %all-to-all-done.got = f32[4,8,8,256]{3,2,1,0:T(8,128)S(1)} async-done(((f32[4,8,8,256]{3,2,1,0:T(8,128)}), f32[4,8,8,256]{3,2,1,0:T(8,128)S(1)}, u32[]{:S(2)}, u32[]{:S(2)}) %all-to-all-start) | async-done | bytes 262176 | tf_op jit(solution)/shard_map/all_to_all | solution.py:273
  31.7 1.0 copy-done.7
  32.8 25.6 %all_to_all.30.got = f32[16,1,128]{2,1,0:T(1,128)S(1)} all-to-all(f32[16,1,128]{2,1,0:T(1,128)S(1)} %get-tuple-element.14), channel_id=1, replica_groups={{0,4,8,12,16,20,24,28,32,36,40,44,48,52,56,60},{1,5,9,13,17,21,25,29,33..., dimensions={0} | all-to-all | bytes 16384 | tf_op jit(solution)/shard_map/all_to_all | solution.py:247
  58.5 1.2 %copy-done.6 = f32[2,8,64,256]{3,2,1,0:T(8,128)S(1)} copy-done((f32[2,8,64,256]{3,2,1,0:T(8,128)S(1)}, f32[2,8,64,256]{3,2,1,0:T(8,128)}, u32[]{:S(2)}) %copy-start.6) | copy-done | bytes 1048600
  59.7 2.8 %shard_map.108.halves = f32[2,4,8,8,256]{4,3,2,1,0:T(8,128)S(1)} custom-call(f32[2,8,64,256]{3,2,1,0:T(8,128)S(1)} %copy-done.6, f32[2,8,64,256]{3,2,1,0:T(8,128)S(1)} %copy-done, f32[8,64,256]{2,1,0:T(8,128)S(1)} %copy-done.3, f32[5,2,64,256]{3,2,1,0:T(8,128)} %collective-permute-done.before, f32[5,2,64,256]{3,2,1,0:T(8,128)} %collective-permute-done.1.after, ...), custom_call_target="tpu_custom_call" | custom-call | flops 10000000 | bytes 6000000 | tf_op jit(solution)/shard_map/pallas_call | solution.py:343
  62.5 5.0 %collective-permute-start.3 = (f32[4,8,8,256]{3,2,1,0:T(8,128)S(1)}, f32[4,8,8,256]{3,2,1,0:T(8,128)S(1)}, u32[]{:S(2)}, u32[]{:S(2)}) collective-permute-start(f32[4,8,8,256]{3,2,1,0:T(8,128)S(1)} %slice_bitcast_fusion), channel_id=1, source_target_pairs={{0,64},{64,0},{128,192},{192,128},{256,320},{320,256},{384,448},{4... | collective-permute-start | bytes 786440 | tf_op jit(solution)/shard_map/ppermute | solution.py:263
  67.5 6.9 %all_to_all.31.peaks = f32[8,1,128]{2,1,0:T(1,128)S(1)} all-to-all(f32[8,1,128]{2,1,0:T(1,128)S(1)} %shard_map.107.order), channel_id=1, replica_groups={{0,1,2,3,64,65,66,67},{4,5,6,7,68,69,70,71},{8,9,10,11,72,73,74,75},{12..., dimensions={0} | all-to-all | bytes 8192 | tf_op jit(solution)/shard_map/all_to_all | solution.py:247
  74.5 8.8 %all_to_all.32.got = f32[4,9,8,256]{3,2,1,0:T(8,128)S(1)} all-to-all(f32[4,9,8,256]{3,2,1,0:T(8,128)S(1)} %shard_map.109), channel_id=1, replica_groups={{0,128,256,384},{64,192,320,448},{1,129,257,385},{65,193,321,449},{2,13..., dimensions={0} | all-to-all | bytes 589824 | tf_op jit(solution)/shard_map/all_to_all | solution.py:273
  83.3 0.2 shard_map.110
  83.4 13.8 %all_to_all.33.got = f32[16,1,256]{2,1,0:T(1,128)S(1)} all-to-all(f32[16,1,256]{2,1,0:T(1,128)S(1)} %get-tuple-element.18), channel_id=1, replica_groups={{0,4,8,12,16,20,24,28,32,36,40,44,48,52,56,60},{1,5,9,13,17,21,25,29,33..., dimensions={0} | all-to-all | bytes 32768 | tf_op jit(solution)/shard_map/all_to_all | solution.py:247
  97.3 12.9 %all_to_all.34.got = f32[32,1,256]{2,1,0:T(1,128)S(1)} all-to-all(f32[32,1,256]{2,1,0:T(1,128)S(1)} %shard_map.111), channel_id=1, replica_groups={{0,1,2,3,64,65,66,67,128,129,130,131,192,193,194,195,256,257,258,259,32..., dimensions={0} | all-to-all | bytes 65536 | tf_op jit(solution)/shard_map/all_to_all | solution.py:247
  110.2 0.7 shard_map.112
  (27 shorter events, 0.2 us)
Async XLA Ops:
  0.6 1.2 %copy-start.1 = (bf16[2,2,8,64,256]{4,3,2,1,0:T(8,128)(2,1)S(1)}, bf16[2,2,8,64,256]{4,3,2,1,0:T(8,128)(2,1)}, u32[]{:S(2)}) copy-start(bf16[2,2,8,64,256]{4,3,2,1,0:T(8,128)(2,1)} %snaps.3) | copy-start | bytes 3145732
  1.9 9.8 %copy-start = (f32[2,8,64,256]{3,2,1,0:T(8,128)S(1)}, f32[2,8,64,256]{3,2,1,0:T(8,128)}, u32[]{:S(2)}) copy-start(f32[2,8,64,256]{3,2,1,0:T(8,128)} %now.3) | copy-start | bytes 3145732
  1.9 9.8 %copy-start.11 = (s32[2,256]{1,0:T(2,128)S(1)}, s32[2,256]{1,0:T(2,128)}, u32[]{:S(2)}) copy-start(s32[2,256]{1,0:T(2,128)} %rec_y.3) | copy-start | bytes 6148
  2.0 9.7 %copy-start.3 = (f32[8,64,256]{2,1,0:T(8,128)S(1)}, f32[8,64,256]{2,1,0:T(8,128)}, u32[]{:S(2)}) copy-start(f32[8,64,256]{2,1,0:T(8,128)} %courant.3) | copy-start | bytes 1572868
  2.7 9.0 %copy-start.8 = (f32[2,2,256]{2,1,0:T(2,128)S(1)}, f32[2,2,256]{2,1,0:T(2,128)}, u32[]{:S(2)}) copy-start(f32[2,2,256]{2,1,0:T(2,128)} %traces.3) | copy-start | bytes 12292
  2.7 17.9 %collective-permute-start.2 = (f32[4,8,8,256]{3,2,1,0:T(8,128)}, f32[4,8,8,256]{3,2,1,0:T(8,128)S(1)}, u32[]{:S(2)}, u32[]{:S(2)}) collective-permute-start(f32[4,8,8,256]{3,2,1,0:T(8,128)} %slice_bitcast_fusion.1), channel_id=1, source_target_pairs={{0,64},{64,0},{128,192},{192,128},{256,320},{320,256},{384,448},{4... | collective-permute-start | bytes 786440 | tf_op jit(solution)/shard_map/ppermute | solution.py:263
  11.7 0.7 copy-start.10
  12.3 1.2 %copy-start.4 = (f32[2,8,64,256]{3,2,1,0:T(8,128)S(1)}, f32[2,8,64,256]{3,2,1,0:T(8,128)}, u32[]{:S(2)}) copy-start(f32[2,8,64,256]{3,2,1,0:T(8,128)} %prev.1) | copy-start | bytes 3145732
  16.0 1.0 copy-start.5
  17.0 41.4 %collective-permute-start = (f32[5,2,64,256]{3,2,1,0:T(8,128)}, f32[5,2,64,256]{3,2,1,0:T(8,128)}, u32[]{:S(2)}, u32[]{:S(2)}) collective-permute-start(f32[5,2,64,256]{3,2,1,0:T(8,128)} %get-tuple-element.12), channel_id=1, source_target_pairs={{0,1},{1,2},{2,3},{3,4},{4,5},{5,6},{6,7},{7,8},{8,9},{9,10},{10,1... | collective-permute-start | bytes 1966088 | tf_op jit(solution)/shard_map/ppermute | solution.py:238
  19.2 39.3 %copy-start.2 = (bf16[2,2,8,64,256]{4,3,2,1,0:T(8,128)(2,1)S(1)}, bf16[2,2,8,64,256]{4,3,2,1,0:T(8,128)(2,1)}, u32[]{:S(2)}) copy-start(bf16[2,2,8,64,256]{4,3,2,1,0:T(8,128)(2,1)} %snaps.3) | copy-start | bytes 3145732
  19.2 39.3 %collective-permute-start.1 = (f32[5,2,64,256]{3,2,1,0:T(8,128)}, f32[5,2,64,256]{3,2,1,0:T(8,128)}, u32[]{:S(2)}, u32[]{:S(2)}) collective-permute-start(f32[5,2,64,256]{3,2,1,0:T(8,128)} %get-tuple-element.13), channel_id=1, source_target_pairs={{1,0},{2,1},{3,2},{4,3},{5,4},{6,5},{7,6},{8,7},{9,8},{10,9},{11,1... | collective-permute-start | bytes 1966088 | tf_op jit(solution)/shard_map/ppermute | solution.py:243
  21.3 10.3 %copy-start.9 = (s32[8,256]{1,0:T(8,128)S(1)}, s32[8,256]{1,0:T(8,128)}, u32[]{:S(2)}) copy-start(s32[8,256]{1,0:T(8,128)} %water.1) | copy-start | bytes 24580
  21.3 10.3 %all-to-all-start = ((f32[4,8,8,256]{3,2,1,0:T(8,128)}), f32[4,8,8,256]{3,2,1,0:T(8,128)S(1)}, u32[]{:S(2)}, u32[]{:S(2)}) async-start(f32[4,8,8,256]{3,2,1,0:T(8,128)} %fusion), calls=%async_computation | async-start | bytes 524288 | tf_op jit(solution)/shard_map/all_to_all | solution.py:273
  31.7 1.0 copy-start.7
  58.5 1.2 %copy-start.6 = (f32[2,8,64,256]{3,2,1,0:T(8,128)S(1)}, f32[2,8,64,256]{3,2,1,0:T(8,128)}, u32[]{:S(2)}) copy-start(f32[2,8,64,256]{3,2,1,0:T(8,128)} %copy-done.5) | copy-start | bytes 3145732
  62.5 11.9 %collective-permute-start.3 = (f32[4,8,8,256]{3,2,1,0:T(8,128)S(1)}, f32[4,8,8,256]{3,2,1,0:T(8,128)S(1)}, u32[]{:S(2)}, u32[]{:S(2)}) collective-permute-start(f32[4,8,8,256]{3,2,1,0:T(8,128)S(1)} %slice_bitcast_fusion), channel_id=1, source_target_pairs={{0,64},{64,0},{128,192},{192,128},{256,320},{320,256},{384,448},{4... | collective-permute-start | bytes 786440 | tf_op jit(solution)/shard_map/ppermute | solution.py:263

commit v3 on v1

--- a/solution.py
+++ b/solution.py
@@ -158,6 +158,15 @@
         for p in range(parts):
             slot = (mine + p % 2) % 2
             out[slot, p // 2, i] = image[p * rows : (p + 1) * rows]
+
+
+def add_kernel(halves, received, traces, rec_x, rec_y, guide, mine, traces_out, x_out, y_out):
+    for c in range(mine.shape[0]):
+        for i in range(mine.shape[1]):
+            mine[c, i] = halves[0, c, i] + received[c, i]
+    traces_out[...] = traces[...]
+    x_out[...] = rec_x[...]
+    y_out[...] = rec_y[...]
 
 
 def folded(line, combine):
@@ -220,6 +229,15 @@
             sums[n, :, k * 128 : (k + 1) * 128] = line
 
 
+def last_kernel(got, value, gradient, sums):
+    gradient[...] = value[...]
+    total = got[0]
+    for n in range(1, got.shape[0]):
+        total = total + got[n]
+    sums[0] = jnp.sum(total[:, :128])
+    sums[1] = jnp.sum(total[:, 128:])
+
+
 def to_next(cells):
     count = lax.axis_size("brick")
     return lax.ppermute(cells, "brick", [(i, i + 1) for i in range(count - 1)])
@@ -248,10 +266,6 @@
 def exchanged(halves):
     parts = lax.axis_size("shot")
     return lax.ppermute(halves[1], "shot", [(i, i ^ 1) for i in range(parts)])
-
-
-def own_rows(halves):
-    return halves[0] + exchanged(halves)
 
 
 def four_chips(pieces):
@@ -295,7 +309,20 @@
         compiler_params=params,
         cost_estimate=pl.CostEstimate(flops=10**6, bytes_accessed=2 * 10**6, transcendentals=0),
     )(forward_snaps, core)
-    illum_mine = own_rows(illum_halves)
+    guide = lax.dynamic_slice_in_dim(direction, offset, rows_part, 1)
+    illum_mine, traces, rec_x, rec_y = pl.pallas_call(
+        add_kernel,
+        out_shape=(
+            shape(halves_shape.shape[1:], f32),
+            shape(traces.shape, f32),
+            shape(rec_x.shape, jnp.int32),
+            shape(rec_y.shape, jnp.int32),
+        ),
+        in_specs=vmem(6),
+        out_specs=tuple(vmem(4)),
+        compiler_params=params,
+        cost_estimate=pl.CostEstimate(flops=10**5, bytes_accessed=10**6, transcendentals=0),
+    )(illum_halves, exchanged(illum_halves), traces, rec_x, rec_y, guide)
     illum_got = four_chips(illum_mine)
 
     illum_part, own_peak = pl.pallas_call(
@@ -350,7 +377,6 @@
     )(image_halves, exchanged(image_halves), peaks)
     image_got = four_chips(pieces)
 
-    guide = lax.dynamic_slice_in_dim(direction, offset, rows_part, 1)
     gradient, sums = pl.pallas_call(
         gradient_kernel,
         out_shape=(shape((cells_x, rows_part, cells_y), f32), shape((len(along[0]), 1, 256), f32)),
@@ -360,8 +386,15 @@
         cost_estimate=pl.CostEstimate(flops=10**6, bytes_accessed=6 * 10**5, transcendentals=0),
     )(image_got, illum_part, water_rows, guide, offset[None])
     sums = fan(jnp.add, swapped(sums, "brick", along), len(across[0]))
-    sums = jnp.sum(swapped(sums, ("shot", "brick"), across), axis=0)
-    return (gradient, jnp.sum(sums.reshape(2, 128), axis=1))
+    gradient, sums = pl.pallas_call(
+        last_kernel,
+        out_shape=(shape(gradient.shape, f32), shape((2,), f32)),
+        in_specs=vmem(2),
+        out_specs=(vmem(1)[0], smem),
+        compiler_params=params,
+        cost_estimate=pl.CostEstimate(flops=10**4, bytes_accessed=2 * 10**5, transcendentals=0),
+    )(swapped(sums, ("shot", "brick"), across), gradient)
+    return (gradient, sums)
 
 
 def solution(mesh):

time: 109 us -> 107 us (0.982)
  blocking collectives: 61.8 us -> 70.3 us
  waiting for transfers between devices: 13.3 us -> 7.4 us
  starting transfers between devices: 24.2 us -> 20.6 us
  other arithmetic: 1.42 us -> 0 us
    all_to_all x0 -> x1, blocking collectives: none -> 8.78 us  [four_chips(): lax.all_to_all(pieces, 'shot', 0, 0, axis_index_groups=groups, tiled=True)]
    all_to_all x2 -> x1, waiting for transfers between devices: 12.1 us -> 6.07 us  [four_chips(): lax.all_to_all(pieces, 'shot', 0, 0, axis_index_groups=groups, tiled=True)]
    all_to_all x2 -> x1, starting transfers between devices: 6.99 us -> 3.54 us  [four_chips(): lax.all_to_all(pieces, 'shot', 0, 0, axis_index_groups=groups, tiled=True)]
  transfers between devices with their start and end apart: 6 -> 5, of which waited for: 3 -> 2; matrix products, arithmetic and copies ran while one was open for 0% -> 0% of each run, Pallas kernels for 0% -> 0%
where the time goes in v3:
time: 107 us; the launch traced here: 106 us
  blocking collectives  70.3 us (66%)
  starting transfers between devices  20.6 us (19%)
  waiting for transfers between devices  7.4 us (7%)
  Pallas kernels  4.17 us (4%)
  local copies, waits for them, and re-layouts  2.76 us (3%)
    all_to_all x4, blocking collectives, swapped(): lax.all_to_all(copies, axis, 0, 0, axis_index_groups=groups, tiled=True)  61.5 us
    ppermute x2, starting transfers between devices, exchanged(): return lax.ppermute(halves[1], 'shot', [(i, i ^ 1) for i in range(parts)])  14.5 us
    all_to_all x1, blocking collectives, four_chips(): lax.all_to_all(pieces, 'shot', 0, 0, axis_index_groups=groups, tiled=True)  8.78 us
    all_to_all x1, waiting for transfers between devices, four_chips(): lax.all_to_all(pieces, 'shot', 0, 0, axis_index_groups=groups, tiled=True)  6.07 us
    all_to_all x1, starting transfers between devices, four_chips(): lax.all_to_all(pieces, 'shot', 0, 0, axis_index_groups=groups, tiled=True)  3.54 us
  transfers between devices with their start and end apart: 5, of which 2 were waited for; matrix products, arithmetic and copies ran while one was open for 0% of the time, Pallas kernels for 0%

profile of v3, /device:TPU:1, one launch (start us, length us, event | category | flops | bytes accessed | tf_op | source)
XLA Modules:
  0.0 106.1 jit_solution(11970712097034010400)
XLA Ops:
  0.6 0.0 copy-start
  0.7 0.0 copy-start.2
  0.7 1.3 %copy-done.2 = bf16[2,2,8,64,256]{4,3,2,1,0:T(8,128)(2,1)S(1)} copy-done((bf16[2,2,8,64,256]{4,3,2,1,0:T(8,128)(2,1)S(1)}, bf16[2,2,8,64,256]{4,3,2,1,0:T(8,128)(2,1)}, u32[]{:S(2)}) %copy-start.2) | copy-done | bytes 1048600
  2.0 0.1 shard_map.104.halves
  2.1 0.0 copy-start.1
  2.1 0.7 slice_bitcast_fusion.1
  2.8 8.8 %collective-permute-start = (f32[4,8,8,256]{3,2,1,0:T(8,128)}, f32[4,8,8,256]{3,2,1,0:T(8,128)S(1)}, u32[]{:S(2)}, u32[]{:S(2)}) collective-permute-start(f32[4,8,8,256]{3,2,1,0:T(8,128)} %slice_bitcast_fusion.1), channel_id=1, source_target_pairs={{0,64},{64,0},{128,192},{192,128},{256,320},{320,256},{384,448},{4... | collective-permute-start | bytes 786440 | tf_op jit(solution)/shard_map/ppermute | solution.py:268
  11.6 1.3 %collective-permute-done.received = f32[4,8,8,256]{3,2,1,0:T(8,128)S(1)} collective-permute-done((f32[4,8,8,256]{3,2,1,0:T(8,128)}, f32[4,8,8,256]{3,2,1,0:T(8,128)S(1)}, u32[]{:S(2)}, u32[]{:S(2)}) %collective-permute-start) | collective-permute-done | bytes 262176 | tf_op jit(solution)/shard_map/ppermute | solution.py:268
  13.0 0.7 copy-done.6
  13.7 3.5 %all-to-all-start = ((f32[4,8,8,256]{3,2,1,0:T(8,128)}), f32[4,8,8,256]{3,2,1,0:T(8,128)S(1)}, u32[]{:S(2)}, u32[]{:S(2)}) async-start(f32[4,8,8,256]{3,2,1,0:T(8,128)} %copy-done.6), calls=%async_computation | async-start | bytes 524288 | tf_op jit(solution)/shard_map/all_to_all | solution.py:274
  17.3 6.1 %all-to-all-done.got = f32[4,8,8,256]{3,2,1,0:T(8,128)S(1)} async-done(((f32[4,8,8,256]{3,2,1,0:T(8,128)}), f32[4,8,8,256]{3,2,1,0:T(8,128)S(1)}, u32[]{:S(2)}, u32[]{:S(2)}) %all-to-all-start) | async-done | bytes 262176 | tf_op jit(solution)/shard_map/all_to_all | solution.py:274
  23.4 0.0 copy-start.3
  23.4 1.5 %shard_map.107 = (f32[2,8,64,256]{3,2,1,0:T(8,128)S(1)}, f32[5,2,64,256]{3,2,1,0:T(8,128)S(1)}, f32[5,2,64,256]{3,2,1,0:T(8,128)S(1)}) custom-call(f32[2,8,64,256]{3,2,1,0:T(8,128)S(1)} %copy-done.5, f32[2,8,64,256]{3,2,1,0:T(8,128)S(1)} %copy-done.1, f32[8,64,256]{2,1,0:T(8,128)S(1)} %copy-done.4, f32[2,2,256]{2,1,0:T(2,128)S(1)} %get-tuple-element.13.traces, ...), custom_call_target="tpu_custom_call" | custom-call | flops 10000000 | bytes 4000000 | tf_op jit(solution)/shard_map/pallas_call | solution.py:342
  24.9 1.3 %collective-permute-start.1 = (f32[5,2,64,256]{3,2,1,0:T(8,128)S(1)}, f32[5,2,64,256]{3,2,1,0:T(8,128)S(1)}, u32[]{:S(2)}, u32[]{:S(2)}) collective-permute-start(f32[5,2,64,256]{3,2,1,0:T(8,128)S(1)} %get-tuple-element.19), channel_id=1, source_target_pairs={{0,1},{1,2},{2,3},{3,4},{4,5},{5,6},{6,7},{7,8},{8,9},{9,10},{10,1... | collective-permute-start | bytes 1966088 | tf_op jit(solution)/shard_map/ppermute | solution.py:243
  26.2 1.3 %collective-permute-start.2 = (f32[5,2,64,256]{3,2,1,0:T(8,128)S(1)}, f32[5,2,64,256]{3,2,1,0:T(8,128)S(1)}, u32[]{:S(2)}, u32[]{:S(2)}) collective-permute-start(f32[5,2,64,256]{3,2,1,0:T(8,128)S(1)} %get-tuple-element.20), channel_id=1, source_target_pairs={{1,0},{2,1},{3,2},{4,3},{5,4},{6,5},{7,6},{8,7},{9,8},{10,9},{11,1... | collective-permute-start | bytes 1966088 | tf_op jit(solution)/shard_map/ppermute | solution.py:248
  27.5 26.9 %all_to_all.30.got = f32[16,1,128]{2,1,0:T(1,128)S(1)} all-to-all(f32[16,1,128]{2,1,0:T(1,128)S(1)} %get-tuple-element.17.order), channel_id=1, replica_groups={{0,4,8,12,16,20,24,28,32,36,40,44,48,52,56,60},{1,5,9,13,17,21,25,29,33..., dimensions={0} | all-to-all | bytes 16384 | tf_op jit(solution)/shard_map/all_to_all | solution.py:252
  54.5 1.6 %shard_map.109.halves = f32[2,4,8,8,256]{4,3,2,1,0:T(8,128)S(1)} custom-call(f32[2,8,64,256]{3,2,1,0:T(8,128)S(1)} %get-tuple-element.18.local, f32[2,8,64,256]{3,2,1,0:T(8,128)S(1)} %copy-done.1, f32[8,64,256]{2,1,0:T(8,128)S(1)} %copy-done.4, f32[5,2,64,256]{3,2,1,0:T(8,128)S(1)} %collective-permute-done.1.before, ...), custom_call_target="tpu_custom_call" | custom-call | flops 10000000 | bytes 6000000 | tf_op jit(solution)/shard_map/pallas_call | solution.py:354
  56.1 5.7 %collective-permute-start.3 = (f32[4,8,8,256]{3,2,1,0:T(8,128)S(1)}, f32[4,8,8,256]{3,2,1,0:T(8,128)S(1)}, u32[]{:S(2)}, u32[]{:S(2)}) collective-permute-start(f32[4,8,8,256]{3,2,1,0:T(8,128)S(1)} %slice_bitcast_fusion), channel_id=1, source_target_pairs={{0,64},{64,0},{128,192},{192,128},{256,320},{320,256},{384,448},{4... | collective-permute-start | bytes 786440 | tf_op jit(solution)/shard_map/ppermute | solution.py:268
  61.9 6.9 %all_to_all.31.peaks = f32[8,1,128]{2,1,0:T(1,128)S(1)} all-to-all(f32[8,1,128]{2,1,0:T(1,128)S(1)} %shard_map.108.order), channel_id=1, replica_groups={{0,1,2,3,64,65,66,67},{4,5,6,7,68,69,70,71},{8,9,10,11,72,73,74,75},{12..., dimensions={0} | all-to-all | bytes 8192 | tf_op jit(solution)/shard_map/all_to_all | solution.py:252
  68.8 8.8 %all_to_all.32.got = f32[4,9,8,256]{3,2,1,0:T(8,128)S(1)} all-to-all(f32[4,9,8,256]{3,2,1,0:T(8,128)S(1)} %shard_map.110), channel_id=1, replica_groups={{0,128,256,384},{64,192,320,448},{1,129,257,385},{65,193,321,449},{2,13..., dimensions={0} | all-to-all | bytes 589824 | tf_op jit(solution)/shard_map/all_to_all | solution.py:274
  77.6 0.2 shard_map.111
  77.8 14.4 %all_to_all.33.got = f32[16,1,256]{2,1,0:T(1,128)S(1)} all-to-all(f32[16,1,256]{2,1,0:T(1,128)S(1)} %get-tuple-element.22), channel_id=1, replica_groups={{0,4,8,12,16,20,24,28,32,36,40,44,48,52,56,60},{1,5,9,13,17,21,25,29,33..., dimensions={0} | all-to-all | bytes 32768 | tf_op jit(solution)/shard_map/all_to_all | solution.py:252
  92.2 13.2 %all_to_all.34.got = f32[32,1,256]{2,1,0:T(1,128)S(1)} all-to-all(f32[32,1,256]{2,1,0:T(1,128)S(1)} %shard_map.112), channel_id=1, replica_groups={{0,1,2,3,64,65,66,67,128,129,130,131,192,193,194,195,256,257,258,259,32..., dimensions={0} | all-to-all | bytes 65536 | tf_op jit(solution)/shard_map/all_to_all | solution.py:252
  105.4 0.7 shard_map.113
  (26 shorter events, 0.2 us)
Async XLA Ops:
  0.6 11.0 %copy-start = (f32[8,64,256]{2,1,0:T(8,128)S(1)}, f32[8,64,256]{2,1,0:T(8,128)}, u32[]{:S(2)}) copy-start(f32[8,64,256]{2,1,0:T(8,128)} %param.17) | copy-start | bytes 1572868
  0.7 1.3 %copy-start.2 = (bf16[2,2,8,64,256]{4,3,2,1,0:T(8,128)(2,1)S(1)}, bf16[2,2,8,64,256]{4,3,2,1,0:T(8,128)(2,1)}, u32[]{:S(2)}) copy-start(bf16[2,2,8,64,256]{4,3,2,1,0:T(8,128)(2,1)} %snaps.3) | copy-start | bytes 3145732
  1.9 11.0 %copy-start.8 = (f32[2,2,256]{2,1,0:T(2,128)S(1)}, f32[2,2,256]{2,1,0:T(2,128)}, u32[]{:S(2)}) copy-start(f32[2,2,256]{2,1,0:T(2,128)} %traces.1) | copy-start | bytes 12292
  1.9 11.0 %copy-start.9 = (s32[2,256]{1,0:T(2,128)S(1)}, s32[2,256]{1,0:T(2,128)}, u32[]{:S(2)}) copy-start(s32[2,256]{1,0:T(2,128)} %rec_x.1) | copy-start | bytes 6148
  1.9 11.0 %copy-start.10 = (s32[2,256]{1,0:T(2,128)S(1)}, s32[2,256]{1,0:T(2,128)}, u32[]{:S(2)}) copy-start(s32[2,256]{1,0:T(2,128)} %rec_y.1) | copy-start | bytes 6148
  1.9 21.4 %copy-start.5 = (f32[2,8,64,256]{3,2,1,0:T(8,128)S(1)}, f32[2,8,64,256]{3,2,1,0:T(8,128)}, u32[]{:S(2)}) copy-start(f32[2,8,64,256]{3,2,1,0:T(8,128)} %prev.1) | copy-start | bytes 3145732
  2.1 21.3 %copy-start.1 = (f32[2,8,64,256]{3,2,1,0:T(8,128)S(1)}, f32[2,8,64,256]{3,2,1,0:T(8,128)}, u32[]{:S(2)}) copy-start(f32[2,8,64,256]{3,2,1,0:T(8,128)} %now.3) | copy-start | bytes 3145732
  2.8 10.1 %collective-permute-start = (f32[4,8,8,256]{3,2,1,0:T(8,128)}, f32[4,8,8,256]{3,2,1,0:T(8,128)S(1)}, u32[]{:S(2)}, u32[]{:S(2)}) collective-permute-start(f32[4,8,8,256]{3,2,1,0:T(8,128)} %slice_bitcast_fusion.1), channel_id=1, source_target_pairs={{0,64},{64,0},{128,192},{192,128},{256,320},{320,256},{384,448},{4... | collective-permute-start | bytes 786440 | tf_op jit(solution)/shard_map/ppermute | solution.py:268
  13.0 0.7 copy-start.6
  13.7 9.7 %copy-start.4 = (f32[8,64,256]{2,1,0:T(8,128)S(1)}, f32[8,64,256]{2,1,0:T(8,128)}, u32[]{:S(2)}) copy-start(f32[8,64,256]{2,1,0:T(8,128)} %courant.3) | copy-start | bytes 1572868
  13.7 9.6 %all-to-all-start = ((f32[4,8,8,256]{3,2,1,0:T(8,128)}), f32[4,8,8,256]{3,2,1,0:T(8,128)S(1)}, u32[]{:S(2)}, u32[]{:S(2)}) async-start(f32[4,8,8,256]{3,2,1,0:T(8,128)} %copy-done.6), calls=%async_computation | async-start | bytes 524288 | tf_op jit(solution)/shard_map/all_to_all | solution.py:274
  23.4 31.1 %copy-start.3 = (bf16[2,2,8,64,256]{4,3,2,1,0:T(8,128)(2,1)S(1)}, bf16[2,2,8,64,256]{4,3,2,1,0:T(8,128)(2,1)}, u32[]{:S(2)}) copy-start(bf16[2,2,8,64,256]{4,3,2,1,0:T(8,128)(2,1)} %snaps.3) | copy-start | bytes 3145732
  24.9 29.6 %collective-permute-start.1 = (f32[5,2,64,256]{3,2,1,0:T(8,128)S(1)}, f32[5,2,64,256]{3,2,1,0:T(8,128)S(1)}, u32[]{:S(2)}, u32[]{:S(2)}) collective-permute-start(f32[5,2,64,256]{3,2,1,0:T(8,128)S(1)} %get-tuple-element.19), channel_id=1, source_target_pairs={{0,1},{1,2},{2,3},{3,4},{4,5},{5,6},{6,7},{7,8},{8,9},{9,10},{10,1... | collective-permute-start | bytes 1966088 | tf_op jit(solution)/shard_map/ppermute | solution.py:243
  26.2 28.3 %collective-permute-start.2 = (f32[5,2,64,256]{3,2,1,0:T(8,128)S(1)}, f32[5,2,64,256]{3,2,1,0:T(8,128)S(1)}, u32[]{:S(2)}, u32[]{:S(2)}) collective-permute-start(f32[5,2,64,256]{3,2,1,0:T(8,128)S(1)} %get-tuple-element.20), channel_id=1, source_target_pairs={{1,0},{2,1},{3,2},{4,3},{5,4},{6,5},{7,6},{8,7},{9,8},{10,9},{11,1... | collective-permute-start | bytes 1966088 | tf_op jit(solution)/shard_map/ppermute | solution.py:248
  56.1 12.7 %collective-permute-start.3 = (f32[4,8,8,256]{3,2,1,0:T(8,128)S(1)}, f32[4,8,8,256]{3,2,1,0:T(8,128)S(1)}, u32[]{:S(2)}, u32[]{:S(2)}) collective-permute-start(f32[4,8,8,256]{3,2,1,0:T(8,128)S(1)} %slice_bitcast_fusion), channel_id=1, source_target_pairs={{0,64},{64,0},{128,192},{192,128},{256,320},{320,256},{384,448},{4... | collective-permute-start | bytes 786440 | tf_op jit(solution)/shard_map/ppermute | solution.py:268
  68.8 8.8 %copy-start.7 = (s32[8,256]{1,0:T(8,128)S(1)}, s32[8,256]{1,0:T(8,128)}, u32[]{:S(2)}) copy-start(s32[8,256]{1,0:T(8,128)} %water.1) | copy-start | bytes 24580

commit v4 on v3

--- a/solution.py
+++ b/solution.py
@@ -63,7 +63,7 @@
     return out
 
 
-def illum_kernel(snaps, core, out):
+def illum_kernel(snaps, core, first_row, first_depth, out):
     shots, steps, planes, depth, width = snaps.shape
     parts = 2 * out.shape[1]
     rows = depth // parts
@@ -79,16 +79,11 @@
             out[slot, p // 2, i] = total[p * rows : (p + 1) * rows]
 
 
-def local_kernel(
-    prev, now, courant, traces, rec_x, rec_y, first_row, order, out, head, tail, plane
-):
+def local_kernel(prev, now, courant, out, head, tail):
     shots, planes, depth, width = now.shape
     band_y = band(width, -90.0)
     band_z = band(depth, 0.0)
     for s in range(shots):
-        plane[...] = injected(
-            traces[s, 0:1], rec_x[s : s + 1], rec_y[s : s + 1], first_row[0], planes, width
-        )
         for i in range(planes):
             v = now[s, i]
             total = in_plane(v, band_z, band_y)
@@ -97,7 +92,6 @@
                     if 0 <= j < planes:
                         total += weight * now[s, j]
             out[s, i] = 2.0 * v - prev[s, i] + courant[i] * (total * (1.0 / 12.0))
-            out[s, i, receiver_depth : receiver_depth + 1] += plane[i : i + 1]
         for j in range(2):
             head[s, j] = out[s, j]
             tail[s, j] = out[s, planes - 2 + j]
@@ -109,8 +103,8 @@
 
 
 def image_kernel(
-    local, now, courant, before, after, snaps,
-    traces, rec_x, rec_y, first_row, core, order, out, first, plane,
+    local, now, courant, before, after, snaps, traces, rec_x, rec_y, first_row, core, order,
+    out, first, injections,
 ):
     shots, planes, depth, width = now.shape
     parts = 2 * out.shape[1]
@@ -120,6 +114,11 @@
     mine = core[0]
     last = planes - 1
     for s in range(shots):
+        for k in range(2):
+            injections[s, k] = injected(
+                traces[s, k : k + 1], rec_x[s : s + 1], rec_y[s : s + 1],
+                first_row[0] - 2, injections.shape[2], width,
+            )
         first[s, 2] = local[s, 0] + courant[0] * (
             far_coef * before[shots + s, 0] + near_coef * before[shots + s, 1]
         )
@@ -138,9 +137,8 @@
             near_coef * now[s, last] + far_coef * now[s, last - 1]
         )
         first[s, planes + 3] = after[s, 1] + after[2 * shots, 1] * (far_coef * now[s, last])
-        plane[s] = injected(
-            traces[s, 1:2], rec_x[s : s + 1], rec_y[s : s + 1], first_row[0], planes, width
-        )
+        for i in range(planes + 4):
+            first[s, i, receiver_depth : receiver_depth + 1] += injections[s, 0, i : i + 1]
     at_level = (
         lax.broadcasted_iota(jnp.int32, (depth, width), 0) == receiver_depth
     )
@@ -152,21 +150,12 @@
             total += 16.0 * (first[s, i + 1] + first[s, i + 3])
             total -= first[s, i] + first[s, i + 4]
             second = 2.0 * v - now[s, i] + courant[i] * (total * (1.0 / 12.0))
-            second += jnp.where(at_level, plane[s, i : i + 1], f32(0.0))
+            second += jnp.where(at_level, injections[s, 1, i + 2 : i + 3], f32(0.0))
             term = snaps[s, 0, i].astype(f32) * v + snaps[s, 1, i].astype(f32) * second
             image = term if image is None else image + term
         for p in range(parts):
             slot = (mine + p % 2) % 2
             out[slot, p // 2, i] = image[p * rows : (p + 1) * rows]
-
-
-def add_kernel(halves, received, traces, rec_x, rec_y, guide, mine, traces_out, x_out, y_out):
-    for c in range(mine.shape[0]):
-        for i in range(mine.shape[1]):
-            mine[c, i] = halves[0, c, i] + received[c, i]
-    traces_out[...] = traces[...]
-    x_out[...] = rec_x[...]
-    y_out[...] = rec_y[...]
 
 
 def folded(line, combine):
@@ -205,12 +194,13 @@
             out[c, planes, :, j : j + 128] = top
 
 
-def gradient_kernel(got, illum, water, guide, first_depth, gradient, sums):
+def gradient_kernel(got, illum, water, direction, first_depth, gradient, sums):
     planes, rows, width = illum.shape
     top = got[0, planes]
     for c in range(1, got.shape[0]):
         top = jnp.maximum(top, got[c, planes])
     peak = jnp.max(top)
+    span = pl.ds(pl.multiple_of(first_depth[0], rows), rows)
     depth = first_depth[0] + lax.broadcasted_iota(jnp.int32, (rows, width), 0)
     square = jnp.zeros((rows, width), f32)
     along = jnp.zeros((rows, width), f32)
@@ -222,7 +212,7 @@
         value = jnp.where(depth >= water[i : i + 1], value, f32(0.0))
         gradient[i] = value
         square += value * value
-        along += value * guide[i]
+        along += value * direction[i, span]
     for k, total in ((0, square), (1, along)):
         line = folded(jnp.sum(total, axis=0, keepdims=True), jnp.add)
         for n in range(sums.shape[0]):
@@ -304,25 +294,12 @@
     illum_halves = pl.pallas_call(
         illum_kernel,
         out_shape=halves_shape,
-        in_specs=vmem(1) + [smem],
+        in_specs=vmem(1) + [smem, smem, smem],
         out_specs=vmem(1)[0],
         compiler_params=params,
         cost_estimate=pl.CostEstimate(flops=10**6, bytes_accessed=2 * 10**6, transcendentals=0),
-    )(forward_snaps, core)
-    guide = lax.dynamic_slice_in_dim(direction, offset, rows_part, 1)
-    illum_mine, traces, rec_x, rec_y = pl.pallas_call(
-        add_kernel,
-        out_shape=(
-            shape(halves_shape.shape[1:], f32),
-            shape(traces.shape, f32),
-            shape(rec_x.shape, jnp.int32),
-            shape(rec_y.shape, jnp.int32),
-        ),
-        in_specs=vmem(6),
-        out_specs=tuple(vmem(4)),
-        compiler_params=params,
-        cost_estimate=pl.CostEstimate(flops=10**5, bytes_accessed=10**6, transcendentals=0),
-    )(illum_halves, exchanged(illum_halves), traces, rec_x, rec_y, guide)
+    )(forward_snaps, core, first_row, offset[None])
+    illum_mine = illum_halves[0] + exchanged(illum_halves)
     illum_got = four_chips(illum_mine)
 
     illum_part, own_peak = pl.pallas_call(
@@ -342,12 +319,11 @@
     local, head, tail = pl.pallas_call(
         local_kernel,
         out_shape=(shape(now.shape, f32), side_shape, side_shape),
-        in_specs=vmem(6) + [smem] + vmem(1),
+        in_specs=vmem(3),
         out_specs=tuple(vmem(3)),
-        scratch_shapes=[pltpu.VMEM((cells_x, cells_y), f32)],
         compiler_params=params,
         cost_estimate=pl.CostEstimate(flops=10**7, bytes_accessed=4 * 10**6, transcendentals=0),
-    )(adjoint_prev, now, courant, traces, rec_x, rec_y, first_row, own_peak)
+    )(adjoint_prev, now, courant)
     before = to_next(tail)
     after = to_previous(head)
 
@@ -358,7 +334,7 @@
         out_specs=vmem(1)[0],
         scratch_shapes=[
             pltpu.VMEM((shots, cells_x + 4, depth_cells, cells_y), f32),
-            pltpu.VMEM((shots, cells_x, cells_y), f32),
+            pltpu.VMEM((shots, 2, cells_x + 8, cells_y), f32),
         ],
         compiler_params=params,
         cost_estimate=pl.CostEstimate(flops=10**7, bytes_accessed=6 * 10**6, transcendentals=0),
@@ -384,7 +360,7 @@
         out_specs=tuple(vmem(2)),
         compiler_params=params,
         cost_estimate=pl.CostEstimate(flops=10**6, bytes_accessed=6 * 10**5, transcendentals=0),
-    )(image_got, illum_part, water_rows, guide, offset[None])
+    )(image_got, illum_part, water_rows, direction, offset[None])
     sums = fan(jnp.add, swapped(sums, "brick", along), len(across[0]))
     gradient, sums = pl.pallas_call(
         last_kernel,

time: 107 us -> 105 us (0.981)
  blocking collectives: 70.3 us -> 78.9 us
  waiting for transfers between devices: 7.4 us -> 0.01 us
  starting transfers between devices: 20.6 us -> 16.8 us
    all_to_all x1 -> x2, blocking collectives: 8.78 us -> 17.8 us  [four_chips(): lax.all_to_all(pieces, 'shot', 0, 0, axis_index_groups=groups, tiled=True)]
    all_to_all x1 -> x0, waiting for transfers between devices: 6.07 us -> none  [four_chips(): lax.all_to_all(pieces, 'shot', 0, 0, axis_index_groups=groups, tiled=True)]
    all_to_all x1 -> x0, starting transfers between devices: 3.54 us -> none  [four_chips(): lax.all_to_all(pieces, 'shot', 0, 0, axis_index_groups=groups, tiled=True)]
    ppermute x2, waiting for transfers between devices: 1.32 us -> 0.01 us  [exchanged(): return lax.ppermute(halves[1], 'shot', [(i, i ^ 1) for i in range(parts)])]
    unnamed x22 -> x20, local copies, waits for them, and re-layouts: 2.01 us -> 3.13 us
  transfers between devices with their start and end apart: 5 -> 4, of which waited for: 2 -> 0; matrix products, arithmetic and copies ran while one was open for 0% -> 0% of each run, Pallas kernels for 0% -> 1%
where the time goes in v4:
time: 105 us; the launch traced here: 104 us
  blocking collectives  78.9 us (75%)
  starting transfers between devices  16.8 us (16%)
  Pallas kernels  4.34 us (4%)
  local copies, waits for them, and re-layouts  3.17 us (3%)
    all_to_all x4, blocking collectives, swapped(): lax.all_to_all(copies, axis, 0, 0, axis_index_groups=groups, tiled=True)  61.1 us
    all_to_all x2, blocking collectives, four_chips(): lax.all_to_all(pieces, 'shot', 0, 0, axis_index_groups=groups, tiled=True)  17.8 us
    ppermute x2, starting transfers between devices, exchanged(): return lax.ppermute(halves[1], 'shot', [(i, i ^ 1) for i in range(parts)])  14 us
    unnamed x20, local copies, waits for them, and re-layouts  3.13 us
  transfers between devices with their start and end apart: 4, of which 0 were waited for; matrix products, arithmetic and copies ran while one was open for 0% of the time, Pallas kernels for 1%

profile of v4, /device:TPU:1, one launch (start us, length us, event | category | flops | bytes accessed | tf_op | source)
XLA Modules:
  0.0 104.0 jit_solution(4562312413282731215)
XLA Ops:
  0.6 0.0 copy-start.1
  0.7 1.2 %copy-done.1 = bf16[2,2,8,64,256]{4,3,2,1,0:T(8,128)(2,1)S(1)} copy-done((bf16[2,2,8,64,256]{4,3,2,1,0:T(8,128)(2,1)S(1)}, bf16[2,2,8,64,256]{4,3,2,1,0:T(8,128)(2,1)}, u32[]{:S(2)}) %copy-start.1) | copy-done | bytes 1048600
  1.9 0.1 shard_map.105
  2.0 0.0 copy-start.3
  2.0 8.9 %collective-permute-start.2 = (f32[4,8,8,256]{3,2,1,0:T(8,128)S(1)}, f32[4,8,8,256]{3,2,1,0:T(8,128)S(1)}, u32[]{:S(2)}, u32[]{:S(2)}) collective-permute-start(f32[4,8,8,256]{3,2,1,0:T(8,128)S(1)} %slice_bitcast_fusion.1), channel_id=1, source_target_pairs={{0,64},{64,0},{128,192},{192,128},{256,320},{320,256},{384,448},{4... | collective-permute-start | bytes 786440 | tf_op jit(solution)/shard_map/ppermute | solution.py:258
  11.0 1.2 %copy-done.4 = f32[2,8,64,256]{3,2,1,0:T(8,128)S(1)} copy-done((f32[2,8,64,256]{3,2,1,0:T(8,128)S(1)}, f32[2,8,64,256]{3,2,1,0:T(8,128)}, u32[]{:S(2)}) %copy-start.4) | copy-done | bytes 1048600
  12.2 1.4 %shard_map.104 = (f32[2,8,64,256]{3,2,1,0:T(8,128)S(1)}, f32[5,2,64,256]{3,2,1,0:T(8,128)S(1)}, f32[5,2,64,256]{3,2,1,0:T(8,128)S(1)}) custom-call(f32[2,8,64,256]{3,2,1,0:T(8,128)S(1)} %copy-done.4, f32[2,8,64,256]{3,2,1,0:T(8,128)S(1)} %copy-done, f32[8,64,256]{2,1,0:T(8,128)S(1)} %copy-done.3), custom_call_target="tpu_custom_call" | custom-call | flops 10000000 | bytes 4000000 | tf_op jit(solution)/shard_map/pallas_call | solution.py:319
  13.6 1.5 %collective-permute-start = (f32[5,2,64,256]{3,2,1,0:T(8,128)S(1)}, f32[5,2,64,256]{3,2,1,0:T(8,128)S(1)}, u32[]{:S(2)}, u32[]{:S(2)}) collective-permute-start(f32[5,2,64,256]{3,2,1,0:T(8,128)S(1)} %get-tuple-element.10), channel_id=1, source_target_pairs={{0,1},{1,2},{2,3},{3,4},{4,5},{5,6},{6,7},{7,8},{8,9},{9,10},{10,1... | collective-permute-start | bytes 1966088 | tf_op jit(solution)/shard_map/ppermute | solution.py:233
  15.1 1.3 %collective-permute-start.1 = (f32[5,2,64,256]{3,2,1,0:T(8,128)S(1)}, f32[5,2,64,256]{3,2,1,0:T(8,128)S(1)}, u32[]{:S(2)}, u32[]{:S(2)}) collective-permute-start(f32[5,2,64,256]{3,2,1,0:T(8,128)S(1)} %get-tuple-element.11), channel_id=1, source_target_pairs={{1,0},{2,1},{3,2},{4,3},{5,4},{6,5},{7,6},{8,7},{9,8},{10,9},{11,1... | collective-permute-start | bytes 1966088 | tf_op jit(solution)/shard_map/ppermute | solution.py:238
  16.5 8.9 %all_to_all.30.got = f32[4,8,8,256]{3,2,1,0:T(8,128)S(1)} all-to-all(f32[4,8,8,256]{3,2,1,0:T(8,128)S(1)} %fusion), channel_id=1, replica_groups={{0,128,256,384},{64,192,320,448},{1,129,257,385},{65,193,321,449},{2,13..., dimensions={0} | all-to-all | bytes 524288 | tf_op jit(solution)/shard_map/all_to_all | solution.py:264
  25.4 27.4 %all_to_all.31.got = f32[16,1,128]{2,1,0:T(1,128)S(1)} all-to-all(f32[16,1,128]{2,1,0:T(1,128)S(1)} %get-tuple-element.12), channel_id=1, replica_groups={{0,4,8,12,16,20,24,28,32,36,40,44,48,52,56,60},{1,5,9,13,17,21,25,29,33..., dimensions={0} | all-to-all | bytes 16384 | tf_op jit(solution)/shard_map/all_to_all | solution.py:242
  52.9 0.6 copy-done.7
  53.5 0.0 copy-done.8
  53.5 0.0 copy-done.9
  53.5 1.8 %shard_map.108.halves = f32[2,4,8,8,256]{4,3,2,1,0:T(8,128)S(1)} custom-call(f32[2,8,64,256]{3,2,1,0:T(8,128)S(1)} %get-tuple-element.9.local, f32[2,8,64,256]{3,2,1,0:T(8,128)S(1)} %copy-done, f32[8,64,256]{2,1,0:T(8,128)S(1)} %copy-done.3, f32[5,2,64,256]{3,2,1,0:T(8,128)S(1)} %collective-permute-done.before, ...), custom_call_target="tpu_custom_call" | custom-call | flops 10000000 | bytes 6000000 | tf_op jit(solution)/shard_map/pallas_call | solution.py:330
  55.4 5.1 %collective-permute-start.3 = (f32[4,8,8,256]{3,2,1,0:T(8,128)S(1)}, f32[4,8,8,256]{3,2,1,0:T(8,128)S(1)}, u32[]{:S(2)}, u32[]{:S(2)}) collective-permute-start(f32[4,8,8,256]{3,2,1,0:T(8,128)S(1)} %slice_bitcast_fusion), channel_id=1, source_target_pairs={{0,64},{64,0},{128,192},{192,128},{256,320},{320,256},{384,448},{4... | collective-permute-start | bytes 786440 | tf_op jit(solution)/shard_map/ppermute | solution.py:258
  60.5 6.9 %all_to_all.32.peaks = f32[8,1,128]{2,1,0:T(1,128)S(1)} all-to-all(f32[8,1,128]{2,1,0:T(1,128)S(1)} %shard_map.107.order), channel_id=1, replica_groups={{0,1,2,3,64,65,66,67},{4,5,6,7,68,69,70,71},{8,9,10,11,72,73,74,75},{12..., dimensions={0} | all-to-all | bytes 8192 | tf_op jit(solution)/shard_map/all_to_all | solution.py:242
  67.5 0.0 copy-start.5
  67.5 0.0 copy-start.6
  67.5 8.9 %all_to_all.33.got = f32[4,9,8,256]{3,2,1,0:T(8,128)S(1)} all-to-all(f32[4,9,8,256]{3,2,1,0:T(8,128)S(1)} %shard_map.109), channel_id=1, replica_groups={{0,128,256,384},{64,192,320,448},{1,129,257,385},{65,193,321,449},{2,13..., dimensions={0} | all-to-all | bytes 589824 | tf_op jit(solution)/shard_map/all_to_all | solution.py:264
  76.4 0.2 shard_map.110
  76.6 13.8 %all_to_all.34.got = f32[16,1,256]{2,1,0:T(1,128)S(1)} all-to-all(f32[16,1,256]{2,1,0:T(1,128)S(1)} %get-tuple-element.14), channel_id=1, replica_groups={{0,4,8,12,16,20,24,28,32,36,40,44,48,52,56,60},{1,5,9,13,17,21,25,29,33..., dimensions={0} | all-to-all | bytes 32768 | tf_op jit(solution)/shard_map/all_to_all | solution.py:242
  90.4 12.9 %all_to_all.35.got = f32[32,1,256]{2,1,0:T(1,128)S(1)} all-to-all(f32[32,1,256]{2,1,0:T(1,128)S(1)} %shard_map.111), channel_id=1, replica_groups={{0,1,2,3,64,65,66,67,128,129,130,131,192,193,194,195,256,257,258,259,32..., dimensions={0} | all-to-all | bytes 65536 | tf_op jit(solution)/shard_map/all_to_all | solution.py:242
  103.4 0.7 shard_map.112
  (22 shorter events, 0.2 us)
Async XLA Ops:
  0.6 1.2 %copy-start.1 = (bf16[2,2,8,64,256]{4,3,2,1,0:T(8,128)(2,1)S(1)}, bf16[2,2,8,64,256]{4,3,2,1,0:T(8,128)(2,1)}, u32[]{:S(2)}) copy-start(bf16[2,2,8,64,256]{4,3,2,1,0:T(8,128)(2,1)} %snaps.3) | copy-start | bytes 3145732
  1.9 9.1 %copy-start = (f32[2,8,64,256]{3,2,1,0:T(8,128)S(1)}, f32[2,8,64,256]{3,2,1,0:T(8,128)}, u32[]{:S(2)}) copy-start(f32[2,8,64,256]{3,2,1,0:T(8,128)} %now.3) | copy-start | bytes 3145732
  2.0 9.0 %copy-start.3 = (f32[8,64,256]{2,1,0:T(8,128)S(1)}, f32[8,64,256]{2,1,0:T(8,128)}, u32[]{:S(2)}) copy-start(f32[8,64,256]{2,1,0:T(8,128)} %courant.3) | copy-start | bytes 1572868
  2.0 14.4 %collective-permute-start.2 = (f32[4,8,8,256]{3,2,1,0:T(8,128)S(1)}, f32[4,8,8,256]{3,2,1,0:T(8,128)S(1)}, u32[]{:S(2)}, u32[]{:S(2)}) collective-permute-start(f32[4,8,8,256]{3,2,1,0:T(8,128)S(1)} %slice_bitcast_fusion.1), channel_id=1, source_target_pairs={{0,64},{64,0},{128,192},{192,128},{256,320},{320,256},{384,448},{4... | collective-permute-start | bytes 786440 | tf_op jit(solution)/shard_map/ppermute | solution.py:258
  11.0 1.2 %copy-start.4 = (f32[2,8,64,256]{3,2,1,0:T(8,128)S(1)}, f32[2,8,64,256]{3,2,1,0:T(8,128)}, u32[]{:S(2)}) copy-start(f32[2,8,64,256]{3,2,1,0:T(8,128)} %prev.1) | copy-start | bytes 3145732
  13.6 39.2 %copy-start.2 = (bf16[2,2,8,64,256]{4,3,2,1,0:T(8,128)(2,1)S(1)}, bf16[2,2,8,64,256]{4,3,2,1,0:T(8,128)(2,1)}, u32[]{:S(2)}) copy-start(bf16[2,2,8,64,256]{4,3,2,1,0:T(8,128)(2,1)} %snaps.3) | copy-start | bytes 3145732
  13.6 39.2 %collective-permute-start = (f32[5,2,64,256]{3,2,1,0:T(8,128)S(1)}, f32[5,2,64,256]{3,2,1,0:T(8,128)S(1)}, u32[]{:S(2)}, u32[]{:S(2)}) collective-permute-start(f32[5,2,64,256]{3,2,1,0:T(8,128)S(1)} %get-tuple-element.10), channel_id=1, source_target_pairs={{0,1},{1,2},{2,3},{3,4},{4,5},{5,6},{6,7},{7,8},{8,9},{9,10},{10,1... | collective-permute-start | bytes 1966088 | tf_op jit(solution)/shard_map/ppermute | solution.py:233
  15.1 37.7 %collective-permute-start.1 = (f32[5,2,64,256]{3,2,1,0:T(8,128)S(1)}, f32[5,2,64,256]{3,2,1,0:T(8,128)S(1)}, u32[]{:S(2)}, u32[]{:S(2)}) collective-permute-start(f32[5,2,64,256]{3,2,1,0:T(8,128)S(1)} %get-tuple-element.11), channel_id=1, source_target_pairs={{1,0},{2,1},{3,2},{4,3},{5,4},{6,5},{7,6},{8,7},{9,8},{10,9},{11,1... | collective-permute-start | bytes 1966088 | tf_op jit(solution)/shard_map/ppermute | solution.py:238
  52.8 0.7 copy-start.7
  52.8 0.7 copy-start.8
  52.8 0.7 copy-start.9
  55.4 12.0 %collective-permute-start.3 = (f32[4,8,8,256]{3,2,1,0:T(8,128)S(1)}, f32[4,8,8,256]{3,2,1,0:T(8,128)S(1)}, u32[]{:S(2)}, u32[]{:S(2)}) collective-permute-start(f32[4,8,8,256]{3,2,1,0:T(8,128)S(1)} %slice_bitcast_fusion), channel_id=1, source_target_pairs={{0,64},{64,0},{128,192},{192,128},{256,320},{320,256},{384,448},{4... | collective-permute-start | bytes 786440 | tf_op jit(solution)/shard_map/ppermute | solution.py:258
  67.5 8.9 %copy-start.5 = (f32[8,64,256]{2,1,0:T(8,128)S(1)}, f32[8,64,256]{2,1,0:T(8,128)}, u32[]{:S(2)}) copy-start(f32[8,64,256]{2,1,0:T(8,128)} %direction.1) | copy-start | bytes 1572868
  67.5 8.9 %copy-start.6 = (s32[8,256]{1,0:T(8,128)S(1)}, s32[8,256]{1,0:T(8,128)}, u32[]{:S(2)}) copy-start(s32[8,256]{1,0:T(8,128)} %water.1) | copy-start | bytes 24580

commit v5 on v4

--- a/solution.py
+++ b/solution.py
@@ -79,7 +79,7 @@
             out[slot, p // 2, i] = total[p * rows : (p + 1) * rows]
 
 
-def local_kernel(prev, now, courant, out, head, tail):
+def local_kernel(now, courant, out):
     shots, planes, depth, width = now.shape
     band_y = band(width, -90.0)
     band_z = band(depth, 0.0)
@@ -91,19 +91,26 @@
                 for j in (i - gap, i + gap):
                     if 0 <= j < planes:
                         total += weight * now[s, j]
-            out[s, i] = 2.0 * v - prev[s, i] + courant[i] * (total * (1.0 / 12.0))
+            out[s, i] = 2.0 * v + courant[i] * (total * (1.0 / 12.0))
+
+
+def edges_kernel(
+    local, prev, now, courant, traces, rec_x, rec_y, head, tail, traces_out, x_out, y_out
+):
+    traces_out[...] = traces[...]
+    x_out[...] = rec_x[...]
+    y_out[...] = rec_y[...]
+    shots, planes, depth, width = now.shape
+    for side, start in ((head, 0), (tail, planes - 2)):
         for j in range(2):
-            head[s, j] = out[s, j]
-            tail[s, j] = out[s, planes - 2 + j]
-            head[shots + s, j] = now[s, j]
-            tail[shots + s, j] = now[s, planes - 2 + j]
-    for j in range(2):
-        head[2 * shots, j] = courant[j]
-        tail[2 * shots, j] = courant[planes - 2 + j]
+            for s in range(shots):
+                side[s, j] = local[s, start + j] - prev[s, start + j]
+                side[shots + s, j] = now[s, start + j]
+            side[2 * shots, j] = courant[start + j]
 
 
 def image_kernel(
-    local, now, courant, before, after, snaps, traces, rec_x, rec_y, first_row, core, order,
+    local, prev, now, courant, before, after, snaps, traces, rec_x, rec_y, first_row, core, order,
     out, first, injections,
 ):
     shots, planes, depth, width = now.shape
@@ -119,14 +126,16 @@
                 traces[s, k : k + 1], rec_x[s : s + 1], rec_y[s : s + 1],
                 first_row[0] - 2, injections.shape[2], width,
             )
-        first[s, 2] = local[s, 0] + courant[0] * (
+        first[s, 2] = local[s, 0] - prev[s, 0] + courant[0] * (
             far_coef * before[shots + s, 0] + near_coef * before[shots + s, 1]
         )
-        first[s, 3] = local[s, 1] + courant[1] * (far_coef * before[shots + s, 1])
+        first[s, 3] = local[s, 1] - prev[s, 1] + courant[1] * (far_coef * before[shots + s, 1])
         for i in range(2, planes - 2):
-            first[s, i + 2] = local[s, i]
-        first[s, planes] = local[s, last - 1] + courant[last - 1] * (far_coef * after[shots + s, 0])
-        first[s, planes + 1] = local[s, last] + courant[last] * (
+            first[s, i + 2] = local[s, i] - prev[s, i]
+        first[s, planes] = local[s, last - 1] - prev[s, last - 1] + courant[last - 1] * (
+            far_coef * after[shots + s, 0]
+        )
+        first[s, planes + 1] = local[s, last] - prev[s, last] + courant[last] * (
             near_coef * after[shots + s, 0] + far_coef * after[shots + s, 1]
         )
         first[s, 0] = before[s, 0] + before[2 * shots, 0] * (far_coef * now[s, 0])
@@ -316,21 +325,35 @@
     peak = fan(jnp.maximum, swapped(own_peak, "brick", along), len(beside[0]))
 
     side_shape = shape((2 * shots + 1, 2, depth_cells, cells_y), f32)
-    local, head, tail = pl.pallas_call(
+    local = pl.pallas_call(
         local_kernel,
-        out_shape=(shape(now.shape, f32), side_shape, side_shape),
-        in_specs=vmem(3),
-        out_specs=tuple(vmem(3)),
+        out_shape=shape(now.shape, f32),
+        in_specs=vmem(2),
+        out_specs=vmem(1)[0],
         compiler_params=params,
         cost_estimate=pl.CostEstimate(flops=10**7, bytes_accessed=4 * 10**6, transcendentals=0),
-    )(adjoint_prev, now, courant)
+    )(now, courant)
+    head, tail, traces, rec_x, rec_y = pl.pallas_call(
+        edges_kernel,
+        out_shape=(
+            side_shape,
+            side_shape,
+            shape(traces.shape, f32),
+            shape(rec_x.shape, jnp.int32),
+            shape(rec_y.shape, jnp.int32),
+        ),
+        in_specs=vmem(7),
+        out_specs=tuple(vmem(5)),
+        compiler_params=params,
+        cost_estimate=pl.CostEstimate(flops=10**5, bytes_accessed=10**6, transcendentals=0),
+    )(local, adjoint_prev, now, courant, traces, rec_x, rec_y)
     before = to_next(tail)
     after = to_previous(head)
 
     image_halves = pl.pallas_call(
         image_kernel,
         out_shape=halves_shape,
-        in_specs=vmem(9) + [smem, smem] + vmem(1),
+        in_specs=vmem(10) + [smem, smem] + vmem(1),
         out_specs=vmem(1)[0],
         scratch_shapes=[
             pltpu.VMEM((shots, cells_x + 4, depth_cells, cells_y), f32),
@@ -339,7 +362,7 @@
         compiler_params=params,
         cost_estimate=pl.CostEstimate(flops=10**7, bytes_accessed=6 * 10**6, transcendentals=0),
     )(
-        local, now, courant, before, after, forward_snaps,
+        local, adjoint_prev, now, courant, before, after, forward_snaps,
         traces, rec_x, rec_y, first_row, core, peak,
     )
     peaks = swapped(peak, ("shot", "brick"), beside)

time: 105 us -> 103 us (0.981)
  local copies, waits for them, and re-layouts: 3.17 us -> 1.31 us
    unnamed x20, local copies, waits for them, and re-layouts: 3.13 us -> 1.27 us
    pallas_call x2 -> x3, Pallas kernels: 3.25 us -> 3.38 us  [the longest x1 1.92 us: per_device(): pl.pallas_call(image_kernel, out_shape=halves_shape, in_specs=vmem(10) +...]
where the time goes in v5:
time: 103 us; the launch traced here: 102 us
  blocking collectives  78.9 us (77%)
  starting transfers between devices  16.8 us (16%)
  Pallas kernels  4.47 us (4%)
  local copies, waits for them, and re-layouts  1.31 us (1%)
    all_to_all x4, blocking collectives, swapped(): lax.all_to_all(copies, axis, 0, 0, axis_index_groups=groups, tiled=True)  61 us
    all_to_all x2, blocking collectives, four_chips(): lax.all_to_all(pieces, 'shot', 0, 0, axis_index_groups=groups, tiled=True)  17.8 us
    ppermute x2, starting transfers between devices, exchanged(): return lax.ppermute(halves[1], 'shot', [(i, i ^ 1) for i in range(parts)])  14 us
  transfers between devices with their start and end apart: 4, of which 0 were waited for; matrix products, arithmetic and copies ran while one was open for 0% of the time, Pallas kernels for 1%

profile of v5, /device:TPU:1, one launch (start us, length us, event | category | flops | bytes accessed | tf_op | source)
XLA Modules:
  0.0 102.4 jit_solution(6616171760162570117)
XLA Ops:
  0.6 0.0 copy-start.3
  0.7 1.2 %copy-done.3 = bf16[2,2,8,64,256]{4,3,2,1,0:T(8,128)(2,1)S(1)} copy-done((bf16[2,2,8,64,256]{4,3,2,1,0:T(8,128)(2,1)S(1)}, bf16[2,2,8,64,256]{4,3,2,1,0:T(8,128)(2,1)}, u32[]{:S(2)}) %copy-start.3) | copy-done | bytes 1048600
  1.9 0.1 shard_map.106
  2.0 0.0 copy-start.1
  2.0 0.0 copy-start.2
  2.1 0.0 copy-start.7
  2.1 0.0 copy-start.8
  2.1 0.0 copy-start.9
  2.1 8.9 %collective-permute-start.2 = (f32[4,8,8,256]{3,2,1,0:T(8,128)S(1)}, f32[4,8,8,256]{3,2,1,0:T(8,128)S(1)}, u32[]{:S(2)}, u32[]{:S(2)}) collective-permute-start(f32[4,8,8,256]{3,2,1,0:T(8,128)S(1)} %slice_bitcast_fusion.1), channel_id=1, source_target_pairs={{0,64},{64,0},{128,192},{192,128},{256,320},{320,256},{384,448},{4... | collective-permute-start | bytes 786440 | tf_op jit(solution)/shard_map/ppermute | solution.py:267
  11.0 1.4 %shard_map.104.local = f32[2,8,64,256]{3,2,1,0:T(8,128)S(1)} custom-call(f32[2,8,64,256]{3,2,1,0:T(8,128)S(1)} %copy-done, f32[8,64,256]{2,1,0:T(8,128)S(1)} %copy-done.1), custom_call_target="tpu_custom_call" | custom-call | flops 10000000 | bytes 4000000 | tf_op jit(solution)/shard_map/pallas_call | solution.py:328
  12.4 0.1 shard_map.105
  12.6 1.5 %collective-permute-start = (f32[5,2,64,256]{3,2,1,0:T(8,128)S(1)}, f32[5,2,64,256]{3,2,1,0:T(8,128)S(1)}, u32[]{:S(2)}, u32[]{:S(2)}) collective-permute-start(f32[5,2,64,256]{3,2,1,0:T(8,128)S(1)} %get-tuple-element.11), channel_id=1, source_target_pairs={{0,1},{1,2},{2,3},{3,4},{4,5},{5,6},{6,7},{7,8},{8,9},{9,10},{10,1... | collective-permute-start | bytes 1966088 | tf_op jit(solution)/shard_map/ppermute | solution.py:242
  14.0 1.3 %collective-permute-start.1 = (f32[5,2,64,256]{3,2,1,0:T(8,128)S(1)}, f32[5,2,64,256]{3,2,1,0:T(8,128)S(1)}, u32[]{:S(2)}, u32[]{:S(2)}) collective-permute-start(f32[5,2,64,256]{3,2,1,0:T(8,128)S(1)} %get-tuple-element.12), channel_id=1, source_target_pairs={{1,0},{2,1},{3,2},{4,3},{5,4},{6,5},{7,6},{8,7},{9,8},{10,9},{11,1... | collective-permute-start | bytes 1966088 | tf_op jit(solution)/shard_map/ppermute | solution.py:247
  15.4 8.9 %all_to_all.30.got = f32[4,8,8,256]{3,2,1,0:T(8,128)S(1)} all-to-all(f32[4,8,8,256]{3,2,1,0:T(8,128)S(1)} %fusion), channel_id=1, replica_groups={{0,128,256,384},{64,192,320,448},{1,129,257,385},{65,193,321,449},{2,13..., dimensions={0} | all-to-all | bytes 524288 | tf_op jit(solution)/shard_map/all_to_all | solution.py:273
  24.4 27.4 %all_to_all.31.got = f32[16,1,128]{2,1,0:T(1,128)S(1)} all-to-all(f32[16,1,128]{2,1,0:T(1,128)S(1)} %get-tuple-element.16), channel_id=1, replica_groups={{0,4,8,12,16,20,24,28,32,36,40,44,48,52,56,60},{1,5,9,13,17,21,25,29,33..., dimensions={0} | all-to-all | bytes 16384 | tf_op jit(solution)/shard_map/all_to_all | solution.py:251
  51.8 1.9 %shard_map.109.halves = f32[2,4,8,8,256]{4,3,2,1,0:T(8,128)S(1)} custom-call(f32[2,8,64,256]{3,2,1,0:T(8,128)S(1)} %shard_map.104.local, f32[2,8,64,256]{3,2,1,0:T(8,128)S(1)} %copy-done.2, f32[2,8,64,256]{3,2,1,0:T(8,128)S(1)} %copy-done, f32[8,64,256]{2,1,0:T(8,128)S(1)} %copy-done.1, f32[5,2,64,256]{3,2,1,0:T(8,128)S(1)} %collective-permute-done.before, ...), custom_call_target="tpu_custom_call" | custom-call | flops 10000000 | bytes 6000000 | tf_op jit(solution)/shard_map/pallas_call | solution.py:353
  53.7 5.1 %collective-permute-start.3 = (f32[4,8,8,256]{3,2,1,0:T(8,128)S(1)}, f32[4,8,8,256]{3,2,1,0:T(8,128)S(1)}, u32[]{:S(2)}, u32[]{:S(2)}) collective-permute-start(f32[4,8,8,256]{3,2,1,0:T(8,128)S(1)} %slice_bitcast_fusion), channel_id=1, source_target_pairs={{0,64},{64,0},{128,192},{192,128},{256,320},{320,256},{384,448},{4... | collective-permute-start | bytes 786440 | tf_op jit(solution)/shard_map/ppermute | solution.py:267
  58.8 6.9 %all_to_all.32.peaks = f32[8,1,128]{2,1,0:T(1,128)S(1)} all-to-all(f32[8,1,128]{2,1,0:T(1,128)S(1)} %shard_map.108.order), channel_id=1, replica_groups={{0,1,2,3,64,65,66,67},{4,5,6,7,68,69,70,71},{8,9,10,11,72,73,74,75},{12..., dimensions={0} | all-to-all | bytes 8192 | tf_op jit(solution)/shard_map/all_to_all | solution.py:251
  65.8 0.0 copy-start.6
  65.8 8.9 %all_to_all.33.got = f32[4,9,8,256]{3,2,1,0:T(8,128)S(1)} all-to-all(f32[4,9,8,256]{3,2,1,0:T(8,128)S(1)} %shard_map.110), channel_id=1, replica_groups={{0,128,256,384},{64,192,320,448},{1,129,257,385},{65,193,321,449},{2,13..., dimensions={0} | all-to-all | bytes 589824 | tf_op jit(solution)/shard_map/all_to_all | solution.py:273
  74.7 0.2 shard_map.111
  74.9 13.8 %all_to_all.34.got = f32[16,1,256]{2,1,0:T(1,128)S(1)} all-to-all(f32[16,1,256]{2,1,0:T(1,128)S(1)} %get-tuple-element.18), channel_id=1, replica_groups={{0,4,8,12,16,20,24,28,32,36,40,44,48,52,56,60},{1,5,9,13,17,21,25,29,33..., dimensions={0} | all-to-all | bytes 32768 | tf_op jit(solution)/shard_map/all_to_all | solution.py:251
  88.8 12.9 %all_to_all.35.got = f32[32,1,256]{2,1,0:T(1,128)S(1)} all-to-all(f32[32,1,256]{2,1,0:T(1,128)S(1)} %shard_map.112), channel_id=1, replica_groups={{0,1,2,3,64,65,66,67,128,129,130,131,192,193,194,195,256,257,258,259,32..., dimensions={0} | all-to-all | bytes 65536 | tf_op jit(solution)/shard_map/all_to_all | solution.py:251
  101.7 0.7 shard_map.113
  (23 shorter events, 0.2 us)
Async XLA Ops:
  0.6 1.2 %copy-start.3 = (bf16[2,2,8,64,256]{4,3,2,1,0:T(8,128)(2,1)S(1)}, bf16[2,2,8,64,256]{4,3,2,1,0:T(8,128)(2,1)}, u32[]{:S(2)}) copy-start(bf16[2,2,8,64,256]{4,3,2,1,0:T(8,128)(2,1)} %snaps.3) | copy-start | bytes 3145732
  1.9 9.2 %copy-start = (f32[2,8,64,256]{3,2,1,0:T(8,128)S(1)}, f32[2,8,64,256]{3,2,1,0:T(8,128)}, u32[]{:S(2)}) copy-start(f32[2,8,64,256]{3,2,1,0:T(8,128)} %now.5) | copy-start | bytes 3145732
  2.0 9.0 %copy-start.1 = (f32[8,64,256]{2,1,0:T(8,128)S(1)}, f32[8,64,256]{2,1,0:T(8,128)}, u32[]{:S(2)}) copy-start(f32[8,64,256]{2,1,0:T(8,128)} %courant.5) | copy-start | bytes 1572868
  2.0 10.4 %copy-start.2 = (f32[2,8,64,256]{3,2,1,0:T(8,128)S(1)}, f32[2,8,64,256]{3,2,1,0:T(8,128)}, u32[]{:S(2)}) copy-start(f32[2,8,64,256]{3,2,1,0:T(8,128)} %prev.3) | copy-start | bytes 3145732
  2.1 10.4 %copy-start.7 = (f32[2,2,256]{2,1,0:T(2,128)S(1)}, f32[2,2,256]{2,1,0:T(2,128)}, u32[]{:S(2)}) copy-start(f32[2,2,256]{2,1,0:T(2,128)} %traces.1) | copy-start | bytes 12292
  2.1 10.4 %copy-start.8 = (s32[2,256]{1,0:T(2,128)S(1)}, s32[2,256]{1,0:T(2,128)}, u32[]{:S(2)}) copy-start(s32[2,256]{1,0:T(2,128)} %rec_x.1) | copy-start | bytes 6148
  2.1 10.4 %copy-start.9 = (s32[2,256]{1,0:T(2,128)S(1)}, s32[2,256]{1,0:T(2,128)}, u32[]{:S(2)}) copy-start(s32[2,256]{1,0:T(2,128)} %rec_y.1) | copy-start | bytes 6148
  2.1 13.2 %collective-permute-start.2 = (f32[4,8,8,256]{3,2,1,0:T(8,128)S(1)}, f32[4,8,8,256]{3,2,1,0:T(8,128)S(1)}, u32[]{:S(2)}, u32[]{:S(2)}) collective-permute-start(f32[4,8,8,256]{3,2,1,0:T(8,128)S(1)} %slice_bitcast_fusion.1), channel_id=1, source_target_pairs={{0,64},{64,0},{128,192},{192,128},{256,320},{320,256},{384,448},{4... | collective-permute-start | bytes 786440 | tf_op jit(solution)/shard_map/ppermute | solution.py:267
  12.6 39.2 %copy-start.4 = (bf16[2,2,8,64,256]{4,3,2,1,0:T(8,128)(2,1)S(1)}, bf16[2,2,8,64,256]{4,3,2,1,0:T(8,128)(2,1)}, u32[]{:S(2)}) copy-start(bf16[2,2,8,64,256]{4,3,2,1,0:T(8,128)(2,1)} %snaps.3) | copy-start | bytes 3145732
  12.6 39.2 %collective-permute-start = (f32[5,2,64,256]{3,2,1,0:T(8,128)S(1)}, f32[5,2,64,256]{3,2,1,0:T(8,128)S(1)}, u32[]{:S(2)}, u32[]{:S(2)}) collective-permute-start(f32[5,2,64,256]{3,2,1,0:T(8,128)S(1)} %get-tuple-element.11), channel_id=1, source_target_pairs={{0,1},{1,2},{2,3},{3,4},{4,5},{5,6},{6,7},{7,8},{8,9},{9,10},{10,1... | collective-permute-start | bytes 1966088 | tf_op jit(solution)/shard_map/ppermute | solution.py:242
  14.0 37.7 %collective-permute-start.1 = (f32[5,2,64,256]{3,2,1,0:T(8,128)S(1)}, f32[5,2,64,256]{3,2,1,0:T(8,128)S(1)}, u32[]{:S(2)}, u32[]{:S(2)}) collective-permute-start(f32[5,2,64,256]{3,2,1,0:T(8,128)S(1)} %get-tuple-element.12), channel_id=1, source_target_pairs={{1,0},{2,1},{3,2},{4,3},{5,4},{6,5},{7,6},{8,7},{9,8},{10,9},{11,1... | collective-permute-start | bytes 1966088 | tf_op jit(solution)/shard_map/ppermute | solution.py:247
  53.7 12.0 %collective-permute-start.3 = (f32[4,8,8,256]{3,2,1,0:T(8,128)S(1)}, f32[4,8,8,256]{3,2,1,0:T(8,128)S(1)}, u32[]{:S(2)}, u32[]{:S(2)}) collective-permute-start(f32[4,8,8,256]{3,2,1,0:T(8,128)S(1)} %slice_bitcast_fusion), channel_id=1, source_target_pairs={{0,64},{64,0},{128,192},{192,128},{256,320},{320,256},{384,448},{4... | collective-permute-start | bytes 786440 | tf_op jit(solution)/shard_map/ppermute | solution.py:267
  65.8 8.9 %copy-start.5 = (f32[8,64,256]{2,1,0:T(8,128)S(1)}, f32[8,64,256]{2,1,0:T(8,128)}, u32[]{:S(2)}) copy-start(f32[8,64,256]{2,1,0:T(8,128)} %direction.1) | copy-start | bytes 1572868
  65.8 8.9 %copy-start.6 = (s32[8,256]{1,0:T(8,128)S(1)}, s32[8,256]{1,0:T(8,128)}, u32[]{:S(2)}) copy-start(s32[8,256]{1,0:T(8,128)} %water.1) | copy-start | bytes 24580

commit v6 on v5

--- a/solution.py
+++ b/solution.py
@@ -39,12 +39,11 @@
 
 
 def in_plane(v, band_z, band_y):
-    high, low = split_two(v)
-    out = jnp.dot(band_z, high, preferred_element_type=f32)
-    out += jnp.dot(band_z, low, preferred_element_type=f32)
-    out += jnp.dot(high, band_y, preferred_element_type=f32)
-    out += jnp.dot(low, band_y, preferred_element_type=f32)
-    return out
+    depth = v.shape[0]
+    both = jnp.concatenate(split_two(v), axis=0)
+    along_y = jnp.dot(both, band_y, preferred_element_type=f32)
+    along_z = jnp.dot(band_z, both, preferred_element_type=f32)
+    return along_z + along_y[:depth] + along_y[depth:]
 
 
 def injected(trace, row_x, row_y, first_row, rows, cells_y):
@@ -82,7 +81,7 @@
 def local_kernel(now, courant, out):
     shots, planes, depth, width = now.shape
     band_y = band(width, -90.0)
-    band_z = band(depth, 0.0)
+    band_z = jnp.concatenate([band(depth, 0.0)] * 2, axis=1)
     for s in range(shots):
         for i in range(planes):
             v = now[s, i]
@@ -117,7 +116,7 @@
     parts = 2 * out.shape[1]
     rows = depth // parts
     band_y = band(width, -90.0)
-    band_z = band(depth, 0.0)
+    band_z = jnp.concatenate([band(depth, 0.0)] * 2, axis=1)
     mine = core[0]
     last = planes - 1
     for s in range(shots):

time: 103 us -> 102 us (level)
  no operation moved by 1% of the time
where the time goes in v6:
time: 102 us
  blocking collectives  78.9 us (77%)
  starting transfers between devices  16.7 us (16%)
  Pallas kernels  3.87 us (4%)
  local copies, waits for them, and re-layouts  1.31 us (1%)
    all_to_all x4, blocking collectives, swapped(): lax.all_to_all(copies, axis, 0, 0, axis_index_groups=groups, tiled=True)  61.1 us
    all_to_all x2, blocking collectives, four_chips(): lax.all_to_all(pieces, 'shot', 0, 0, axis_index_groups=groups, tiled=True)  17.9 us
    ppermute x2, starting transfers between devices, exchanged(): return lax.ppermute(halves[1], 'shot', [(i, i ^ 1) for i in range(parts)])  14 us
  transfers between devices with their start and end apart: 4, of which 0 were waited for; matrix products, arithmetic and copies ran while one was open for 0% of the time, Pallas kernels for 1%

profile of v6, /device:TPU:1, one launch (start us, length us, event | category | flops | bytes accessed | tf_op | source)
XLA Modules:
  0.0 101.8 jit_solution(17129010374966711258)
XLA Ops:
  0.6 0.0 copy-start.3
  0.7 1.2 %copy-done.3 = bf16[2,2,8,64,256]{4,3,2,1,0:T(8,128)(2,1)S(1)} copy-done((bf16[2,2,8,64,256]{4,3,2,1,0:T(8,128)(2,1)S(1)}, bf16[2,2,8,64,256]{4,3,2,1,0:T(8,128)(2,1)}, u32[]{:S(2)}) %copy-start.3) | copy-done | bytes 1048600
  1.9 0.1 shard_map.106
  2.0 0.0 copy-start.1
  2.0 0.0 copy-start.2
  2.1 0.0 copy-start.7
  2.1 0.0 copy-start.8
  2.1 8.9 %collective-permute-start.2 = (f32[4,8,8,256]{3,2,1,0:T(8,128)S(1)}, f32[4,8,8,256]{3,2,1,0:T(8,128)S(1)}, u32[]{:S(2)}, u32[]{:S(2)}) collective-permute-start(f32[4,8,8,256]{3,2,1,0:T(8,128)S(1)} %slice_bitcast_fusion.1), channel_id=1, source_target_pairs={{0,64},{64,0},{128,192},{192,128},{256,320},{320,256},{384,448},{4... | collective-permute-start | bytes 786440 | tf_op jit(solution)/shard_map/ppermute | solution.py:266
  11.0 1.1 %shard_map.104.local = f32[2,8,64,256]{3,2,1,0:T(8,128)S(1)} custom-call(f32[2,8,64,256]{3,2,1,0:T(8,128)S(1)} %copy-done, f32[8,64,256]{2,1,0:T(8,128)S(1)} %copy-done.1), custom_call_target="tpu_custom_call" | custom-call | flops 10000000 | bytes 4000000 | tf_op jit(solution)/shard_map/pallas_call | solution.py:327
  12.2 0.1 shard_map.105
  12.3 0.0 copy-start.4
  12.3 1.5 %collective-permute-start = (f32[5,2,64,256]{3,2,1,0:T(8,128)S(1)}, f32[5,2,64,256]{3,2,1,0:T(8,128)S(1)}, u32[]{:S(2)}, u32[]{:S(2)}) collective-permute-start(f32[5,2,64,256]{3,2,1,0:T(8,128)S(1)} %get-tuple-element.11), channel_id=1, source_target_pairs={{0,1},{1,2},{2,3},{3,4},{4,5},{5,6},{6,7},{7,8},{8,9},{9,10},{10,1... | collective-permute-start | bytes 1966088 | tf_op jit(solution)/shard_map/ppermute | solution.py:241
  13.8 1.3 %collective-permute-start.1 = (f32[5,2,64,256]{3,2,1,0:T(8,128)S(1)}, f32[5,2,64,256]{3,2,1,0:T(8,128)S(1)}, u32[]{:S(2)}, u32[]{:S(2)}) collective-permute-start(f32[5,2,64,256]{3,2,1,0:T(8,128)S(1)} %get-tuple-element.12), channel_id=1, source_target_pairs={{1,0},{2,1},{3,2},{4,3},{5,4},{6,5},{7,6},{8,7},{9,8},{10,9},{11,1... | collective-permute-start | bytes 1966088 | tf_op jit(solution)/shard_map/ppermute | solution.py:246
  15.1 8.9 %all_to_all.30.got = f32[4,8,8,256]{3,2,1,0:T(8,128)S(1)} all-to-all(f32[4,8,8,256]{3,2,1,0:T(8,128)S(1)} %fusion), channel_id=1, replica_groups={{0,128,256,384},{64,192,320,448},{1,129,257,385},{65,193,321,449},{2,13..., dimensions={0} | all-to-all | bytes 524288 | tf_op jit(solution)/shard_map/all_to_all | solution.py:272
  24.1 27.4 %all_to_all.31.got = f32[16,1,128]{2,1,0:T(1,128)S(1)} all-to-all(f32[16,1,128]{2,1,0:T(1,128)S(1)} %get-tuple-element.16), channel_id=1, replica_groups={{0,4,8,12,16,20,24,28,32,36,40,44,48,52,56,60},{1,5,9,13,17,21,25,29,33..., dimensions={0} | all-to-all | bytes 16384 | tf_op jit(solution)/shard_map/all_to_all | solution.py:250
  51.5 1.6 %shard_map.109.halves = f32[2,4,8,8,256]{4,3,2,1,0:T(8,128)S(1)} custom-call(f32[2,8,64,256]{3,2,1,0:T(8,128)S(1)} %shard_map.104.local, f32[2,8,64,256]{3,2,1,0:T(8,128)S(1)} %copy-done.2, f32[2,8,64,256]{3,2,1,0:T(8,128)S(1)} %copy-done, f32[8,64,256]{2,1,0:T(8,128)S(1)} %copy-done.1, f32[5,2,64,256]{3,2,1,0:T(8,128)S(1)} %collective-permute-done.before, ...), custom_call_target="tpu_custom_call" | custom-call | flops 10000000 | bytes 6000000 | tf_op jit(solution)/shard_map/pallas_call | solution.py:352
  53.2 5.1 %collective-permute-start.3 = (f32[4,8,8,256]{3,2,1,0:T(8,128)S(1)}, f32[4,8,8,256]{3,2,1,0:T(8,128)S(1)}, u32[]{:S(2)}, u32[]{:S(2)}) collective-permute-start(f32[4,8,8,256]{3,2,1,0:T(8,128)S(1)} %slice_bitcast_fusion), channel_id=1, source_target_pairs={{0,64},{64,0},{128,192},{192,128},{256,320},{320,256},{384,448},{4... | collective-permute-start | bytes 786440 | tf_op jit(solution)/shard_map/ppermute | solution.py:266
  58.2 6.9 %all_to_all.32.peaks = f32[8,1,128]{2,1,0:T(1,128)S(1)} all-to-all(f32[8,1,128]{2,1,0:T(1,128)S(1)} %shard_map.108.order), channel_id=1, replica_groups={{0,1,2,3,64,65,66,67},{4,5,6,7,68,69,70,71},{8,9,10,11,72,73,74,75},{12..., dimensions={0} | all-to-all | bytes 8192 | tf_op jit(solution)/shard_map/all_to_all | solution.py:250
  65.2 0.0 copy-start.6
  65.2 8.9 %all_to_all.33.got = f32[4,9,8,256]{3,2,1,0:T(8,128)S(1)} all-to-all(f32[4,9,8,256]{3,2,1,0:T(8,128)S(1)} %shard_map.110), channel_id=1, replica_groups={{0,128,256,384},{64,192,320,448},{1,129,257,385},{65,193,321,449},{2,13..., dimensions={0} | all-to-all | bytes 589824 | tf_op jit(solution)/shard_map/all_to_all | solution.py:272
  74.2 0.2 shard_map.111
  74.3 13.8 %all_to_all.34.got = f32[16,1,256]{2,1,0:T(1,128)S(1)} all-to-all(f32[16,1,256]{2,1,0:T(1,128)S(1)} %get-tuple-element.18), channel_id=1, replica_groups={{0,4,8,12,16,20,24,28,32,36,40,44,48,52,56,60},{1,5,9,13,17,21,25,29,33..., dimensions={0} | all-to-all | bytes 32768 | tf_op jit(solution)/shard_map/all_to_all | solution.py:250
  88.2 12.9 %all_to_all.35.got = f32[32,1,256]{2,1,0:T(1,128)S(1)} all-to-all(f32[32,1,256]{2,1,0:T(1,128)S(1)} %shard_map.112), channel_id=1, replica_groups={{0,1,2,3,64,65,66,67,128,129,130,131,192,193,194,195,256,257,258,259,32..., dimensions={0} | all-to-all | bytes 65536 | tf_op jit(solution)/shard_map/all_to_all | solution.py:250
  101.1 0.7 shard_map.113
  (23 shorter events, 0.2 us)
Async XLA Ops:
  0.6 1.2 %copy-start.3 = (bf16[2,2,8,64,256]{4,3,2,1,0:T(8,128)(2,1)S(1)}, bf16[2,2,8,64,256]{4,3,2,1,0:T(8,128)(2,1)}, u32[]{:S(2)}) copy-start(bf16[2,2,8,64,256]{4,3,2,1,0:T(8,128)(2,1)} %snaps.3) | copy-start | bytes 3145732
  1.9 9.2 %copy-start = (f32[2,8,64,256]{3,2,1,0:T(8,128)S(1)}, f32[2,8,64,256]{3,2,1,0:T(8,128)}, u32[]{:S(2)}) copy-start(f32[2,8,64,256]{3,2,1,0:T(8,128)} %now.5) | copy-start | bytes 3145732
  2.0 9.0 %copy-start.1 = (f32[8,64,256]{2,1,0:T(8,128)S(1)}, f32[8,64,256]{2,1,0:T(8,128)}, u32[]{:S(2)}) copy-start(f32[8,64,256]{2,1,0:T(8,128)} %courant.5) | copy-start | bytes 1572868
  2.0 10.1 %copy-start.2 = (f32[2,8,64,256]{3,2,1,0:T(8,128)S(1)}, f32[2,8,64,256]{3,2,1,0:T(8,128)}, u32[]{:S(2)}) copy-start(f32[2,8,64,256]{3,2,1,0:T(8,128)} %prev.3) | copy-start | bytes 3145732
  2.1 10.1 %copy-start.7 = (f32[2,2,256]{2,1,0:T(2,128)S(1)}, f32[2,2,256]{2,1,0:T(2,128)}, u32[]{:S(2)}) copy-start(f32[2,2,256]{2,1,0:T(2,128)} %traces.1) | copy-start | bytes 12292
  2.1 10.1 %copy-start.8 = (s32[2,256]{1,0:T(2,128)S(1)}, s32[2,256]{1,0:T(2,128)}, u32[]{:S(2)}) copy-start(s32[2,256]{1,0:T(2,128)} %rec_x.1) | copy-start | bytes 6148
  2.1 10.1 %copy-start.9 = (s32[2,256]{1,0:T(2,128)S(1)}, s32[2,256]{1,0:T(2,128)}, u32[]{:S(2)}) copy-start(s32[2,256]{1,0:T(2,128)} %rec_y.1) | copy-start | bytes 6148
  2.1 13.0 %collective-permute-start.2 = (f32[4,8,8,256]{3,2,1,0:T(8,128)S(1)}, f32[4,8,8,256]{3,2,1,0:T(8,128)S(1)}, u32[]{:S(2)}, u32[]{:S(2)}) collective-permute-start(f32[4,8,8,256]{3,2,1,0:T(8,128)S(1)} %slice_bitcast_fusion.1), channel_id=1, source_target_pairs={{0,64},{64,0},{128,192},{192,128},{256,320},{320,256},{384,448},{4... | collective-permute-start | bytes 786440 | tf_op jit(solution)/shard_map/ppermute | solution.py:266
  12.3 39.2 %copy-start.4 = (bf16[2,2,8,64,256]{4,3,2,1,0:T(8,128)(2,1)S(1)}, bf16[2,2,8,64,256]{4,3,2,1,0:T(8,128)(2,1)}, u32[]{:S(2)}) copy-start(bf16[2,2,8,64,256]{4,3,2,1,0:T(8,128)(2,1)} %snaps.3) | copy-start | bytes 3145732
  12.3 39.2 %collective-permute-start = (f32[5,2,64,256]{3,2,1,0:T(8,128)S(1)}, f32[5,2,64,256]{3,2,1,0:T(8,128)S(1)}, u32[]{:S(2)}, u32[]{:S(2)}) collective-permute-start(f32[5,2,64,256]{3,2,1,0:T(8,128)S(1)} %get-tuple-element.11), channel_id=1, source_target_pairs={{0,1},{1,2},{2,3},{3,4},{4,5},{5,6},{6,7},{7,8},{8,9},{9,10},{10,1... | collective-permute-start | bytes 1966088 | tf_op jit(solution)/shard_map/ppermute | solution.py:241
  13.8 37.7 %collective-permute-start.1 = (f32[5,2,64,256]{3,2,1,0:T(8,128)S(1)}, f32[5,2,64,256]{3,2,1,0:T(8,128)S(1)}, u32[]{:S(2)}, u32[]{:S(2)}) collective-permute-start(f32[5,2,64,256]{3,2,1,0:T(8,128)S(1)} %get-tuple-element.12), channel_id=1, source_target_pairs={{1,0},{2,1},{3,2},{4,3},{5,4},{6,5},{7,6},{8,7},{9,8},{10,9},{11,1... | collective-permute-start | bytes 1966088 | tf_op jit(solution)/shard_map/ppermute | solution.py:246
  53.2 12.0 %collective-permute-start.3 = (f32[4,8,8,256]{3,2,1,0:T(8,128)S(1)}, f32[4,8,8,256]{3,2,1,0:T(8,128)S(1)}, u32[]{:S(2)}, u32[]{:S(2)}) collective-permute-start(f32[4,8,8,256]{3,2,1,0:T(8,128)S(1)} %slice_bitcast_fusion), channel_id=1, source_target_pairs={{0,64},{64,0},{128,192},{192,128},{256,320},{320,256},{384,448},{4... | collective-permute-start | bytes 786440 | tf_op jit(solution)/shard_map/ppermute | solution.py:266
  65.2 8.9 %copy-start.5 = (f32[8,64,256]{2,1,0:T(8,128)S(1)}, f32[8,64,256]{2,1,0:T(8,128)}, u32[]{:S(2)}) copy-start(f32[8,64,256]{2,1,0:T(8,128)} %direction.1) | copy-start | bytes 1572868
  65.2 8.9 %copy-start.6 = (s32[8,256]{1,0:T(8,128)S(1)}, s32[8,256]{1,0:T(8,128)}, u32[]{:S(2)}) copy-start(s32[8,256]{1,0:T(8,128)} %water.1) | copy-start | bytes 24580

commit v7 on v6

--- a/solution.py
+++ b/solution.py
@@ -221,10 +221,12 @@
         gradient[i] = value
         square += value * value
         along += value * direction[i, span]
-    for k, total in ((0, square), (1, along)):
-        line = folded(jnp.sum(total, axis=0, keepdims=True), jnp.add)
-        for n in range(sums.shape[0]):
-            sums[n, :, k * 128 : (k + 1) * 128] = line
+    square, along = (folded(total, jnp.add) for total in (square, along))
+    square, along = (total + pltpu.roll(total, 64, 1) for total in (square, along))
+    lane = lax.broadcasted_iota(jnp.int32, square.shape, 1)
+    line = jnp.sum(jnp.where(lane < 64, square, along), axis=0, keepdims=True)
+    for n in range(sums.shape[0]):
+        sums[n] = line
 
 
 def last_kernel(got, value, gradient, sums):
@@ -232,8 +234,9 @@
     total = got[0]
     for n in range(1, got.shape[0]):
         total = total + got[n]
-    sums[0] = jnp.sum(total[:, :128])
-    sums[1] = jnp.sum(total[:, 128:])
+    lane = lax.broadcasted_iota(jnp.int32, total.shape, 1)
+    sums[0] = jnp.sum(jnp.where(lane < 64, total, f32(0.0)))
+    sums[1] = jnp.sum(jnp.where(lane < 64, f32(0.0), total))
 
 
 def to_next(cells):
@@ -377,7 +380,7 @@
 
     gradient, sums = pl.pallas_call(
         gradient_kernel,
-        out_shape=(shape((cells_x, rows_part, cells_y), f32), shape((len(along[0]), 1, 256), f32)),
+        out_shape=(shape((cells_x, rows_part, cells_y), f32), shape((len(along[0]), 1, 128), f32)),
         in_specs=vmem(4) + [smem],
         out_specs=tuple(vmem(2)),
         compiler_params=params,

time: 102 us -> 102 us (level)
  no operation moved by 1% of the time
where the time goes in v7:
time: 102 us
  blocking collectives  78.6 us (77%)
  starting transfers between devices  16.7 us (16%)
  Pallas kernels  3.93 us (4%)
  local copies, waits for them, and re-layouts  1.31 us (1%)
    all_to_all x4, blocking collectives, swapped(): lax.all_to_all(copies, axis, 0, 0, axis_index_groups=groups, tiled=True)  60.8 us
    all_to_all x2, blocking collectives, four_chips(): lax.all_to_all(pieces, 'shot', 0, 0, axis_index_groups=groups, tiled=True)  17.9 us
    ppermute x2, starting transfers between devices, exchanged(): return lax.ppermute(halves[1], 'shot', [(i, i ^ 1) for i in range(parts)])  14 us
  transfers between devices with their start and end apart: 4, of which 0 were waited for; matrix products, arithmetic and copies ran while one was open for 0% of the time, Pallas kernels for 1%

profile of v7, /device:TPU:1, one launch (start us, length us, event | category | flops | bytes accessed | tf_op | source)
XLA Modules:
  0.0 101.5 jit_solution(1942953977517739756)
XLA Ops:
  0.6 0.0 copy-start.3
  0.7 1.2 %copy-done.3 = bf16[2,2,8,64,256]{4,3,2,1,0:T(8,128)(2,1)S(1)} copy-done((bf16[2,2,8,64,256]{4,3,2,1,0:T(8,128)(2,1)S(1)}, bf16[2,2,8,64,256]{4,3,2,1,0:T(8,128)(2,1)}, u32[]{:S(2)}) %copy-start.3) | copy-done | bytes 1048600
  1.9 0.1 shard_map.106
  2.0 0.0 copy-start.1
  2.0 0.0 copy-start.2
  2.1 0.0 copy-start.7
  2.1 0.0 copy-start.8
  2.1 8.9 %collective-permute-start.2 = (f32[4,8,8,256]{3,2,1,0:T(8,128)S(1)}, f32[4,8,8,256]{3,2,1,0:T(8,128)S(1)}, u32[]{:S(2)}, u32[]{:S(2)}) collective-permute-start(f32[4,8,8,256]{3,2,1,0:T(8,128)S(1)} %slice_bitcast_fusion.1), channel_id=1, source_target_pairs={{0,64},{64,0},{128,192},{192,128},{256,320},{320,256},{384,448},{4... | collective-permute-start | bytes 786440 | tf_op jit(solution)/shard_map/ppermute | solution.py:269
  11.0 1.1 %shard_map.104.local = f32[2,8,64,256]{3,2,1,0:T(8,128)S(1)} custom-call(f32[2,8,64,256]{3,2,1,0:T(8,128)S(1)} %copy-done, f32[8,64,256]{2,1,0:T(8,128)S(1)} %copy-done.1), custom_call_target="tpu_custom_call" | custom-call | flops 10000000 | bytes 4000000 | tf_op jit(solution)/shard_map/pallas_call | solution.py:330
  12.2 0.1 shard_map.105
  12.3 0.0 copy-start.4
  12.3 1.5 %collective-permute-start = (f32[5,2,64,256]{3,2,1,0:T(8,128)S(1)}, f32[5,2,64,256]{3,2,1,0:T(8,128)S(1)}, u32[]{:S(2)}, u32[]{:S(2)}) collective-permute-start(f32[5,2,64,256]{3,2,1,0:T(8,128)S(1)} %get-tuple-element.11), channel_id=1, source_target_pairs={{0,1},{1,2},{2,3},{3,4},{4,5},{5,6},{6,7},{7,8},{8,9},{9,10},{10,1... | collective-permute-start | bytes 1966088 | tf_op jit(solution)/shard_map/ppermute | solution.py:244
  13.8 1.3 %collective-permute-start.1 = (f32[5,2,64,256]{3,2,1,0:T(8,128)S(1)}, f32[5,2,64,256]{3,2,1,0:T(8,128)S(1)}, u32[]{:S(2)}, u32[]{:S(2)}) collective-permute-start(f32[5,2,64,256]{3,2,1,0:T(8,128)S(1)} %get-tuple-element.12), channel_id=1, source_target_pairs={{1,0},{2,1},{3,2},{4,3},{5,4},{6,5},{7,6},{8,7},{9,8},{10,9},{11,1... | collective-permute-start | bytes 1966088 | tf_op jit(solution)/shard_map/ppermute | solution.py:249
  15.1 8.9 %all_to_all.30.got = f32[4,8,8,256]{3,2,1,0:T(8,128)S(1)} all-to-all(f32[4,8,8,256]{3,2,1,0:T(8,128)S(1)} %fusion), channel_id=1, replica_groups={{0,128,256,384},{64,192,320,448},{1,129,257,385},{65,193,321,449},{2,13..., dimensions={0} | all-to-all | bytes 524288 | tf_op jit(solution)/shard_map/all_to_all | solution.py:275
  24.1 27.4 %all_to_all.31.got = f32[16,1,128]{2,1,0:T(1,128)S(1)} all-to-all(f32[16,1,128]{2,1,0:T(1,128)S(1)} %get-tuple-element.16), channel_id=1, replica_groups={{0,4,8,12,16,20,24,28,32,36,40,44,48,52,56,60},{1,5,9,13,17,21,25,29,33..., dimensions={0} | all-to-all | bytes 16384 | tf_op jit(solution)/shard_map/all_to_all | solution.py:253
  51.5 1.6 %shard_map.109.halves = f32[2,4,8,8,256]{4,3,2,1,0:T(8,128)S(1)} custom-call(f32[2,8,64,256]{3,2,1,0:T(8,128)S(1)} %shard_map.104.local, f32[2,8,64,256]{3,2,1,0:T(8,128)S(1)} %copy-done.2, f32[2,8,64,256]{3,2,1,0:T(8,128)S(1)} %copy-done, f32[8,64,256]{2,1,0:T(8,128)S(1)} %copy-done.1, f32[5,2,64,256]{3,2,1,0:T(8,128)S(1)} %collective-permute-done.before, ...), custom_call_target="tpu_custom_call" | custom-call | flops 10000000 | bytes 6000000 | tf_op jit(solution)/shard_map/pallas_call | solution.py:355
  53.2 5.1 %collective-permute-start.3 = (f32[4,8,8,256]{3,2,1,0:T(8,128)S(1)}, f32[4,8,8,256]{3,2,1,0:T(8,128)S(1)}, u32[]{:S(2)}, u32[]{:S(2)}) collective-permute-start(f32[4,8,8,256]{3,2,1,0:T(8,128)S(1)} %slice_bitcast_fusion), channel_id=1, source_target_pairs={{0,64},{64,0},{128,192},{192,128},{256,320},{320,256},{384,448},{4... | collective-permute-start | bytes 786440 | tf_op jit(solution)/shard_map/ppermute | solution.py:269
  58.2 6.9 %all_to_all.32.peaks = f32[8,1,128]{2,1,0:T(1,128)S(1)} all-to-all(f32[8,1,128]{2,1,0:T(1,128)S(1)} %shard_map.108.order), channel_id=1, replica_groups={{0,1,2,3,64,65,66,67},{4,5,6,7,68,69,70,71},{8,9,10,11,72,73,74,75},{12..., dimensions={0} | all-to-all | bytes 8192 | tf_op jit(solution)/shard_map/all_to_all | solution.py:253
  65.2 0.0 copy-start.6
  65.2 8.9 %all_to_all.33.got = f32[4,9,8,256]{3,2,1,0:T(8,128)S(1)} all-to-all(f32[4,9,8,256]{3,2,1,0:T(8,128)S(1)} %shard_map.110), channel_id=1, replica_groups={{0,128,256,384},{64,192,320,448},{1,129,257,385},{65,193,321,449},{2,13..., dimensions={0} | all-to-all | bytes 589824 | tf_op jit(solution)/shard_map/all_to_all | solution.py:275
  74.2 0.2 shard_map.111
  74.4 13.8 %all_to_all.34.got = f32[16,1,128]{2,1,0:T(1,128)S(1)} all-to-all(f32[16,1,128]{2,1,0:T(1,128)S(1)} %get-tuple-element.18), channel_id=1, replica_groups={{0,4,8,12,16,20,24,28,32,36,40,44,48,52,56,60},{1,5,9,13,17,21,25,29,33..., dimensions={0} | all-to-all | bytes 16384 | tf_op jit(solution)/shard_map/all_to_all | solution.py:253
  88.2 12.6 %all_to_all.35.got = f32[32,1,128]{2,1,0:T(1,128)S(1)} all-to-all(f32[32,1,128]{2,1,0:T(1,128)S(1)} %shard_map.112), channel_id=1, replica_groups={{0,1,2,3,64,65,66,67,128,129,130,131,192,193,194,195,256,257,258,259,32..., dimensions={0} | all-to-all | bytes 32768 | tf_op jit(solution)/shard_map/all_to_all | solution.py:253
  100.9 0.7 shard_map.113
  (23 shorter events, 0.2 us)
Async XLA Ops:
  0.6 1.2 %copy-start.3 = (bf16[2,2,8,64,256]{4,3,2,1,0:T(8,128)(2,1)S(1)}, bf16[2,2,8,64,256]{4,3,2,1,0:T(8,128)(2,1)}, u32[]{:S(2)}) copy-start(bf16[2,2,8,64,256]{4,3,2,1,0:T(8,128)(2,1)} %snaps.3) | copy-start | bytes 3145732
  1.9 9.2 %copy-start = (f32[2,8,64,256]{3,2,1,0:T(8,128)S(1)}, f32[2,8,64,256]{3,2,1,0:T(8,128)}, u32[]{:S(2)}) copy-start(f32[2,8,64,256]{3,2,1,0:T(8,128)} %now.5) | copy-start | bytes 3145732
  2.0 9.0 %copy-start.1 = (f32[8,64,256]{2,1,0:T(8,128)S(1)}, f32[8,64,256]{2,1,0:T(8,128)}, u32[]{:S(2)}) copy-start(f32[8,64,256]{2,1,0:T(8,128)} %courant.5) | copy-start | bytes 1572868
  2.0 10.1 %copy-start.2 = (f32[2,8,64,256]{3,2,1,0:T(8,128)S(1)}, f32[2,8,64,256]{3,2,1,0:T(8,128)}, u32[]{:S(2)}) copy-start(f32[2,8,64,256]{3,2,1,0:T(8,128)} %prev.3) | copy-start | bytes 3145732
  2.1 10.1 %copy-start.7 = (f32[2,2,256]{2,1,0:T(2,128)S(1)}, f32[2,2,256]{2,1,0:T(2,128)}, u32[]{:S(2)}) copy-start(f32[2,2,256]{2,1,0:T(2,128)} %traces.1) | copy-start | bytes 12292
  2.1 10.1 %copy-start.8 = (s32[2,256]{1,0:T(2,128)S(1)}, s32[2,256]{1,0:T(2,128)}, u32[]{:S(2)}) copy-start(s32[2,256]{1,0:T(2,128)} %rec_x.1) | copy-start | bytes 6148
  2.1 10.1 %copy-start.9 = (s32[2,256]{1,0:T(2,128)S(1)}, s32[2,256]{1,0:T(2,128)}, u32[]{:S(2)}) copy-start(s32[2,256]{1,0:T(2,128)} %rec_y.1) | copy-start | bytes 6148
  2.1 13.0 %collective-permute-start.2 = (f32[4,8,8,256]{3,2,1,0:T(8,128)S(1)}, f32[4,8,8,256]{3,2,1,0:T(8,128)S(1)}, u32[]{:S(2)}, u32[]{:S(2)}) collective-permute-start(f32[4,8,8,256]{3,2,1,0:T(8,128)S(1)} %slice_bitcast_fusion.1), channel_id=1, source_target_pairs={{0,64},{64,0},{128,192},{192,128},{256,320},{320,256},{384,448},{4... | collective-permute-start | bytes 786440 | tf_op jit(solution)/shard_map/ppermute | solution.py:269
  12.3 39.2 %copy-start.4 = (bf16[2,2,8,64,256]{4,3,2,1,0:T(8,128)(2,1)S(1)}, bf16[2,2,8,64,256]{4,3,2,1,0:T(8,128)(2,1)}, u32[]{:S(2)}) copy-start(bf16[2,2,8,64,256]{4,3,2,1,0:T(8,128)(2,1)} %snaps.3) | copy-start | bytes 3145732
  12.3 39.2 %collective-permute-start = (f32[5,2,64,256]{3,2,1,0:T(8,128)S(1)}, f32[5,2,64,256]{3,2,1,0:T(8,128)S(1)}, u32[]{:S(2)}, u32[]{:S(2)}) collective-permute-start(f32[5,2,64,256]{3,2,1,0:T(8,128)S(1)} %get-tuple-element.11), channel_id=1, source_target_pairs={{0,1},{1,2},{2,3},{3,4},{4,5},{5,6},{6,7},{7,8},{8,9},{9,10},{10,1... | collective-permute-start | bytes 1966088 | tf_op jit(solution)/shard_map/ppermute | solution.py:244
  13.8 37.7 %collective-permute-start.1 = (f32[5,2,64,256]{3,2,1,0:T(8,128)S(1)}, f32[5,2,64,256]{3,2,1,0:T(8,128)S(1)}, u32[]{:S(2)}, u32[]{:S(2)}) collective-permute-start(f32[5,2,64,256]{3,2,1,0:T(8,128)S(1)} %get-tuple-element.12), channel_id=1, source_target_pairs={{1,0},{2,1},{3,2},{4,3},{5,4},{6,5},{7,6},{8,7},{9,8},{10,9},{11,1... | collective-permute-start | bytes 1966088 | tf_op jit(solution)/shard_map/ppermute | solution.py:249
  53.2 12.0 %collective-permute-start.3 = (f32[4,8,8,256]{3,2,1,0:T(8,128)S(1)}, f32[4,8,8,256]{3,2,1,0:T(8,128)S(1)}, u32[]{:S(2)}, u32[]{:S(2)}) collective-permute-start(f32[4,8,8,256]{3,2,1,0:T(8,128)S(1)} %slice_bitcast_fusion), channel_id=1, source_target_pairs={{0,64},{64,0},{128,192},{192,128},{256,320},{320,256},{384,448},{4... | collective-permute-start | bytes 786440 | tf_op jit(solution)/shard_map/ppermute | solution.py:269
  65.2 8.9 %copy-start.5 = (f32[8,64,256]{2,1,0:T(8,128)S(1)}, f32[8,64,256]{2,1,0:T(8,128)}, u32[]{:S(2)}) copy-start(f32[8,64,256]{2,1,0:T(8,128)} %direction.1) | copy-start | bytes 1572868
  65.2 8.9 %copy-start.6 = (s32[8,256]{1,0:T(8,128)S(1)}, s32[8,256]{1,0:T(8,128)}, u32[]{:S(2)}) copy-start(s32[8,256]{1,0:T(8,128)} %water.1) | copy-start | bytes 24580

commit v8 on v6

--- a/solution.py
+++ b/solution.py
@@ -377,13 +377,13 @@
 
     gradient, sums = pl.pallas_call(
         gradient_kernel,
-        out_shape=(shape((cells_x, rows_part, cells_y), f32), shape((len(along[0]), 1, 256), f32)),
+        out_shape=(shape((cells_x, rows_part, cells_y), f32), shape((len(across[0]), 1, 256), f32)),
         in_specs=vmem(4) + [smem],
         out_specs=tuple(vmem(2)),
         compiler_params=params,
         cost_estimate=pl.CostEstimate(flops=10**6, bytes_accessed=6 * 10**5, transcendentals=0),
     )(image_got, illum_part, water_rows, direction, offset[None])
-    sums = fan(jnp.add, swapped(sums, "brick", along), len(across[0]))
+    sums = fan(jnp.add, swapped(sums, ("shot", "brick"), across), len(along[0]))
     gradient, sums = pl.pallas_call(
         last_kernel,
         out_shape=(shape(gradient.shape, f32), shape((2,), f32)),
@@ -391,7 +391,7 @@
         out_specs=(vmem(1)[0], smem),
         compiler_params=params,
         cost_estimate=pl.CostEstimate(flops=10**4, bytes_accessed=2 * 10**5, transcendentals=0),
-    )(swapped(sums, ("shot", "brick"), across), gradient)
+    )(swapped(sums, "brick", along), gradient)
     return (gradient, sums)
 
 

time: 102 us -> 101 us (level)
  blocking collectives: 78.9 us -> 77.8 us
    all_to_all x4, blocking collectives: 61.1 us -> 59.9 us  [swapped(): lax.all_to_all(copies, axis, 0, 0, axis_index_groups=groups, tiled=True)]
where the time goes in v8:
time: 101 us
  blocking collectives  77.8 us (77%)
  starting transfers between devices  16.7 us (17%)
  Pallas kernels  3.88 us (4%)
  local copies, waits for them, and re-layouts  1.31 us (1%)
    all_to_all x4, blocking collectives, swapped(): lax.all_to_all(copies, axis, 0, 0, axis_index_groups=groups, tiled=True)  59.9 us
    all_to_all x2, blocking collectives, four_chips(): lax.all_to_all(pieces, 'shot', 0, 0, axis_index_groups=groups, tiled=True)  17.9 us
    ppermute x2, starting transfers between devices, exchanged(): return lax.ppermute(halves[1], 'shot', [(i, i ^ 1) for i in range(parts)])  14 us
  transfers between devices with their start and end apart: 4, of which 0 were waited for; matrix products, arithmetic and copies ran while one was open for 0% of the time, Pallas kernels for 1%

profile of v8, /device:TPU:1, one launch (start us, length us, event | category | flops | bytes accessed | tf_op | source)
XLA Modules:
  0.0 100.7 jit_solution(711488506028692144)
XLA Ops:
  0.6 0.0 copy-start.3
  0.7 1.2 %copy-done.3 = bf16[2,2,8,64,256]{4,3,2,1,0:T(8,128)(2,1)S(1)} copy-done((bf16[2,2,8,64,256]{4,3,2,1,0:T(8,128)(2,1)S(1)}, bf16[2,2,8,64,256]{4,3,2,1,0:T(8,128)(2,1)}, u32[]{:S(2)}) %copy-start.3) | copy-done | bytes 1048600
  1.9 0.1 shard_map.106
  2.0 0.0 copy-start.1
  2.0 0.0 copy-start.2
  2.1 0.0 copy-start.7
  2.1 0.0 copy-start.8
  2.1 8.9 %collective-permute-start.2 = (f32[4,8,8,256]{3,2,1,0:T(8,128)S(1)}, f32[4,8,8,256]{3,2,1,0:T(8,128)S(1)}, u32[]{:S(2)}, u32[]{:S(2)}) collective-permute-start(f32[4,8,8,256]{3,2,1,0:T(8,128)S(1)} %slice_bitcast_fusion.1), channel_id=1, source_target_pairs={{0,64},{64,0},{128,192},{192,128},{256,320},{320,256},{384,448},{4... | collective-permute-start | bytes 786440 | tf_op jit(solution)/shard_map/ppermute | solution.py:266
  11.0 1.1 %shard_map.104.local = f32[2,8,64,256]{3,2,1,0:T(8,128)S(1)} custom-call(f32[2,8,64,256]{3,2,1,0:T(8,128)S(1)} %copy-done, f32[8,64,256]{2,1,0:T(8,128)S(1)} %copy-done.1), custom_call_target="tpu_custom_call" | custom-call | flops 10000000 | bytes 4000000 | tf_op jit(solution)/shard_map/pallas_call | solution.py:327
  12.2 0.1 shard_map.105
  12.3 0.0 copy-start.4
  12.3 1.5 %collective-permute-start = (f32[5,2,64,256]{3,2,1,0:T(8,128)S(1)}, f32[5,2,64,256]{3,2,1,0:T(8,128)S(1)}, u32[]{:S(2)}, u32[]{:S(2)}) collective-permute-start(f32[5,2,64,256]{3,2,1,0:T(8,128)S(1)} %get-tuple-element.11), channel_id=1, source_target_pairs={{0,1},{1,2},{2,3},{3,4},{4,5},{5,6},{6,7},{7,8},{8,9},{9,10},{10,1... | collective-permute-start | bytes 1966088 | tf_op jit(solution)/shard_map/ppermute | solution.py:241
  13.8 1.3 %collective-permute-start.1 = (f32[5,2,64,256]{3,2,1,0:T(8,128)S(1)}, f32[5,2,64,256]{3,2,1,0:T(8,128)S(1)}, u32[]{:S(2)}, u32[]{:S(2)}) collective-permute-start(f32[5,2,64,256]{3,2,1,0:T(8,128)S(1)} %get-tuple-element.12), channel_id=1, source_target_pairs={{1,0},{2,1},{3,2},{4,3},{5,4},{6,5},{7,6},{8,7},{9,8},{10,9},{11,1... | collective-permute-start | bytes 1966088 | tf_op jit(solution)/shard_map/ppermute | solution.py:246
  15.1 8.9 %all_to_all.30.got = f32[4,8,8,256]{3,2,1,0:T(8,128)S(1)} all-to-all(f32[4,8,8,256]{3,2,1,0:T(8,128)S(1)} %fusion), channel_id=1, replica_groups={{0,128,256,384},{64,192,320,448},{1,129,257,385},{65,193,321,449},{2,13..., dimensions={0} | all-to-all | bytes 524288 | tf_op jit(solution)/shard_map/all_to_all | solution.py:272
  24.1 27.4 %all_to_all.31.got = f32[16,1,128]{2,1,0:T(1,128)S(1)} all-to-all(f32[16,1,128]{2,1,0:T(1,128)S(1)} %get-tuple-element.16), channel_id=1, replica_groups={{0,4,8,12,16,20,24,28,32,36,40,44,48,52,56,60},{1,5,9,13,17,21,25,29,33..., dimensions={0} | all-to-all | bytes 16384 | tf_op jit(solution)/shard_map/all_to_all | solution.py:250
  51.5 1.6 %shard_map.109.halves = f32[2,4,8,8,256]{4,3,2,1,0:T(8,128)S(1)} custom-call(f32[2,8,64,256]{3,2,1,0:T(8,128)S(1)} %shard_map.104.local, f32[2,8,64,256]{3,2,1,0:T(8,128)S(1)} %copy-done.2, f32[2,8,64,256]{3,2,1,0:T(8,128)S(1)} %copy-done, f32[8,64,256]{2,1,0:T(8,128)S(1)} %copy-done.1, f32[5,2,64,256]{3,2,1,0:T(8,128)S(1)} %collective-permute-done.before, ...), custom_call_target="tpu_custom_call" | custom-call | flops 10000000 | bytes 6000000 | tf_op jit(solution)/shard_map/pallas_call | solution.py:352
  53.2 5.1 %collective-permute-start.3 = (f32[4,8,8,256]{3,2,1,0:T(8,128)S(1)}, f32[4,8,8,256]{3,2,1,0:T(8,128)S(1)}, u32[]{:S(2)}, u32[]{:S(2)}) collective-permute-start(f32[4,8,8,256]{3,2,1,0:T(8,128)S(1)} %slice_bitcast_fusion), channel_id=1, source_target_pairs={{0,64},{64,0},{128,192},{192,128},{256,320},{320,256},{384,448},{4... | collective-permute-start | bytes 786440 | tf_op jit(solution)/shard_map/ppermute | solution.py:266
  58.2 6.9 %all_to_all.32.peaks = f32[8,1,128]{2,1,0:T(1,128)S(1)} all-to-all(f32[8,1,128]{2,1,0:T(1,128)S(1)} %shard_map.108.order), channel_id=1, replica_groups={{0,1,2,3,64,65,66,67},{4,5,6,7,68,69,70,71},{8,9,10,11,72,73,74,75},{12..., dimensions={0} | all-to-all | bytes 8192 | tf_op jit(solution)/shard_map/all_to_all | solution.py:250
  65.2 0.0 copy-start.6
  65.2 8.9 %all_to_all.33.got = f32[4,9,8,256]{3,2,1,0:T(8,128)S(1)} all-to-all(f32[4,9,8,256]{3,2,1,0:T(8,128)S(1)} %shard_map.110), channel_id=1, replica_groups={{0,128,256,384},{64,192,320,448},{1,129,257,385},{65,193,321,449},{2,13..., dimensions={0} | all-to-all | bytes 589824 | tf_op jit(solution)/shard_map/all_to_all | solution.py:272
  74.2 0.2 shard_map.111
  74.3 11.8 %all_to_all.34.got = f32[32,1,256]{2,1,0:T(1,128)S(1)} all-to-all(f32[32,1,256]{2,1,0:T(1,128)S(1)} %get-tuple-element.18), channel_id=1, replica_groups={{0,1,2,3,64,65,66,67,128,129,130,131,192,193,194,195,256,257,258,259,32..., dimensions={0} | all-to-all | bytes 65536 | tf_op jit(solution)/shard_map/all_to_all | solution.py:250
  86.2 13.9 %all_to_all.35.got = f32[16,1,256]{2,1,0:T(1,128)S(1)} all-to-all(f32[16,1,256]{2,1,0:T(1,128)S(1)} %shard_map.112), channel_id=1, replica_groups={{0,4,8,12,16,20,24,28,32,36,40,44,48,52,56,60},{1,5,9,13,17,21,25,29,33..., dimensions={0} | all-to-all | bytes 32768 | tf_op jit(solution)/shard_map/all_to_all | solution.py:250
  100.0 0.7 shard_map.113
  (23 shorter events, 0.2 us)
Async XLA Ops:
  0.6 1.2 %copy-start.3 = (bf16[2,2,8,64,256]{4,3,2,1,0:T(8,128)(2,1)S(1)}, bf16[2,2,8,64,256]{4,3,2,1,0:T(8,128)(2,1)}, u32[]{:S(2)}) copy-start(bf16[2,2,8,64,256]{4,3,2,1,0:T(8,128)(2,1)} %snaps.3) | copy-start | bytes 3145732
  1.9 9.2 %copy-start = (f32[2,8,64,256]{3,2,1,0:T(8,128)S(1)}, f32[2,8,64,256]{3,2,1,0:T(8,128)}, u32[]{:S(2)}) copy-start(f32[2,8,64,256]{3,2,1,0:T(8,128)} %now.5) | copy-start | bytes 3145732
  2.0 9.0 %copy-start.1 = (f32[8,64,256]{2,1,0:T(8,128)S(1)}, f32[8,64,256]{2,1,0:T(8,128)}, u32[]{:S(2)}) copy-start(f32[8,64,256]{2,1,0:T(8,128)} %courant.5) | copy-start | bytes 1572868
  2.0 10.1 %copy-start.2 = (f32[2,8,64,256]{3,2,1,0:T(8,128)S(1)}, f32[2,8,64,256]{3,2,1,0:T(8,128)}, u32[]{:S(2)}) copy-start(f32[2,8,64,256]{3,2,1,0:T(8,128)} %prev.3) | copy-start | bytes 3145732
  2.1 10.1 %copy-start.7 = (f32[2,2,256]{2,1,0:T(2,128)S(1)}, f32[2,2,256]{2,1,0:T(2,128)}, u32[]{:S(2)}) copy-start(f32[2,2,256]{2,1,0:T(2,128)} %traces.1) | copy-start | bytes 12292
  2.1 10.1 %copy-start.8 = (s32[2,256]{1,0:T(2,128)S(1)}, s32[2,256]{1,0:T(2,128)}, u32[]{:S(2)}) copy-start(s32[2,256]{1,0:T(2,128)} %rec_x.1) | copy-start | bytes 6148
  2.1 10.1 %copy-start.9 = (s32[2,256]{1,0:T(2,128)S(1)}, s32[2,256]{1,0:T(2,128)}, u32[]{:S(2)}) copy-start(s32[2,256]{1,0:T(2,128)} %rec_y.1) | copy-start | bytes 6148
  2.1 13.0 %collective-permute-start.2 = (f32[4,8,8,256]{3,2,1,0:T(8,128)S(1)}, f32[4,8,8,256]{3,2,1,0:T(8,128)S(1)}, u32[]{:S(2)}, u32[]{:S(2)}) collective-permute-start(f32[4,8,8,256]{3,2,1,0:T(8,128)S(1)} %slice_bitcast_fusion.1), channel_id=1, source_target_pairs={{0,64},{64,0},{128,192},{192,128},{256,320},{320,256},{384,448},{4... | collective-permute-start | bytes 786440 | tf_op jit(solution)/shard_map/ppermute | solution.py:266
  12.3 39.2 %copy-start.4 = (bf16[2,2,8,64,256]{4,3,2,1,0:T(8,128)(2,1)S(1)}, bf16[2,2,8,64,256]{4,3,2,1,0:T(8,128)(2,1)}, u32[]{:S(2)}) copy-start(bf16[2,2,8,64,256]{4,3,2,1,0:T(8,128)(2,1)} %snaps.3) | copy-start | bytes 3145732
  12.3 39.2 %collective-permute-start = (f32[5,2,64,256]{3,2,1,0:T(8,128)S(1)}, f32[5,2,64,256]{3,2,1,0:T(8,128)S(1)}, u32[]{:S(2)}, u32[]{:S(2)}) collective-permute-start(f32[5,2,64,256]{3,2,1,0:T(8,128)S(1)} %get-tuple-element.11), channel_id=1, source_target_pairs={{0,1},{1,2},{2,3},{3,4},{4,5},{5,6},{6,7},{7,8},{8,9},{9,10},{10,1... | collective-permute-start | bytes 1966088 | tf_op jit(solution)/shard_map/ppermute | solution.py:241
  13.8 37.7 %collective-permute-start.1 = (f32[5,2,64,256]{3,2,1,0:T(8,128)S(1)}, f32[5,2,64,256]{3,2,1,0:T(8,128)S(1)}, u32[]{:S(2)}, u32[]{:S(2)}) collective-permute-start(f32[5,2,64,256]{3,2,1,0:T(8,128)S(1)} %get-tuple-element.12), channel_id=1, source_target_pairs={{1,0},{2,1},{3,2},{4,3},{5,4},{6,5},{7,6},{8,7},{9,8},{10,9},{11,1... | collective-permute-start | bytes 1966088 | tf_op jit(solution)/shard_map/ppermute | solution.py:246
  53.2 12.0 %collective-permute-start.3 = (f32[4,8,8,256]{3,2,1,0:T(8,128)S(1)}, f32[4,8,8,256]{3,2,1,0:T(8,128)S(1)}, u32[]{:S(2)}, u32[]{:S(2)}) collective-permute-start(f32[4,8,8,256]{3,2,1,0:T(8,128)S(1)} %slice_bitcast_fusion), channel_id=1, source_target_pairs={{0,64},{64,0},{128,192},{192,128},{256,320},{320,256},{384,448},{4... | collective-permute-start | bytes 786440 | tf_op jit(solution)/shard_map/ppermute | solution.py:266
  65.2 8.9 %copy-start.5 = (f32[8,64,256]{2,1,0:T(8,128)S(1)}, f32[8,64,256]{2,1,0:T(8,128)}, u32[]{:S(2)}) copy-start(f32[8,64,256]{2,1,0:T(8,128)} %direction.1) | copy-start | bytes 1572868
  65.2 8.9 %copy-start.6 = (s32[8,256]{1,0:T(8,128)S(1)}, s32[8,256]{1,0:T(8,128)}, u32[]{:S(2)}) copy-start(s32[8,256]{1,0:T(8,128)} %water.1) | copy-start | bytes 24580
